TPU v7x, 256 devices: a whole 4x4x8 slice. The times are simulated.
256 devices in a mesh: feat: 8 (over z), clus: 32 (over y, x, core).
Axes of the slice: x: 4, y: 4, z: 8, core: 2. Of those that a mesh axis runs over, the one named last changes fastest.
Arguments:
- embeddings: bfloat16 [196608, 2048], P('clus', 'feat')
- signs: int32 [2048], P('feat'), may hold values from 0 to 1
- coords: int32 [512], replicated, may hold values from 0 to 2047, as said below
- cluster: int32 [196608], P('clus'), may hold values from 0 to 4095, as said below
- order: int32 [196608], P('clus'), may hold values from 0 to 196607, each once
Outputs:
- best: float32 [32, 6144], P('clus', 'feat')
Inputs may be any that keep to these rules, and one draw needn't show every extreme that they name: Clusters belong to owners: cluster c belongs to owner c // 16. Among the 768 rows of each aligned block (rows of one device) at most 12 belong to one owner's clusters, and one owner receives exactly 12 rows from every block. `coords`: the sampled coordinates are distinct.
All inputs are finite; a program needn't handle non-finite values.
Results may differ from a plain program's by a relative error of at most 0.00035.
Values may be sent and summed in bfloat16 or wider, within the bound.
A program may use at most 128 MiB of HBM per device.

v0:
```python
import jax
import jax.numpy as jnp
import numpy as np
from jax import lax
from jax.sharding import PartitionSpec as P

CL_OWN = 16


def walsh_table(count, dtype):
    index = np.arange(count)
    table = np.ones((count, count))
    for level in range(count.bit_length() - 1):
        both = (index[:, None] >> level & 1) * (index[None, :] >> level & 1)
        table = table * np.where(both == 1, -1.0, 1.0)
    return jnp.asarray(table, dtype)


def compare_rows(keys, key_cluster, key_order):
    total = keys.shape[0]
    block = 512
    steps = total // block

    def one_block(pieces):
        queries, groups, places = pieces
        scores = lax.dot_general(
            queries, keys, (((1,), (1,)), ((), ())), preferred_element_type=jnp.float32
        )
        mask = (
            (key_cluster[None, :] == groups[:, None])
            & (key_order[None, :] < places[:, None])
            & (key_cluster[None, :] >= 0)
        )
        return jnp.max(jnp.where(mask, scores, jnp.float32(0.0)), axis=1)

    parts_in = (
        keys.reshape(steps, block, keys.shape[1]),
        key_cluster.reshape(steps, block),
        key_order.reshape(steps, block),
    )
    return lax.map(one_block, parts_in).reshape(total)


def local(embeddings, signs, coords, cluster, order):
    feat_count = lax.axis_size("feat")
    clus_count = lax.axis_size("clus")
    owners = feat_count * clus_count
    rows_here = embeddings.shape[0] // feat_count
    width = embeddings.shape[1]
    total_dim = width * feat_count
    keep = coords.shape[0]
    capacity = 4 * rows_here // owners
    sign_row = (2 * signs - 1).astype(jnp.bfloat16)
    signed = embeddings * sign_row[None, :]
    inner = walsh_table(width, jnp.bfloat16)
    feat_index = lax.axis_index("feat")
    moved = lax.all_to_all(signed, "feat", split_axis=0, concat_axis=1, tiled=True)
    blocks = moved.reshape(rows_here, feat_count, width)
    partial_value = jnp.einsum("rab,bc->rac", blocks, inner, preferred_element_type=jnp.float32)
    outer = walsh_table(feat_count, jnp.float32)
    spread = jnp.einsum(
        "rab,ad->rdb", partial_value, outer, precision=lax.Precision.HIGHEST
    ).reshape(rows_here, total_dim)
    sketch = jnp.take(spread, coords, axis=1)
    total_sq = jnp.sum(sketch * sketch, axis=1, keepdims=True)
    unit = (sketch * lax.rsqrt(total_sq + 1e-06)).astype(jnp.bfloat16)
    mine = lax.dynamic_slice_in_dim(cluster, feat_index * rows_here, rows_here, 0)
    places = lax.dynamic_slice_in_dim(order, feat_index * rows_here, rows_here, 0)
    owner = mine // CL_OWN
    onehot = (owner[:, None] == jnp.arange(owners, dtype=jnp.int32)[None, :]).astype(jnp.bfloat16)
    line = jnp.arange(rows_here, dtype=jnp.int32)
    earlier = (line[:, None] > line[None, :]).astype(jnp.bfloat16)
    before = jnp.dot(earlier, onehot, preferred_element_type=jnp.float32)
    position = jnp.sum(before * onehot.astype(jnp.float32), axis=1).astype(jnp.int32)
    slot = owner * capacity + position
    sent = jnp.zeros((owners * capacity, keep), jnp.bfloat16).at[slot].set(unit)
    sent_cluster = jnp.full((owners * capacity,), -1, jnp.int32).at[slot].set(mine)
    sent_order = jnp.zeros((owners * capacity,), jnp.int32).at[slot].set(places)
    sent = sent.reshape(feat_count, clus_count, capacity, keep)
    sent_cluster = sent_cluster.reshape(feat_count, clus_count, capacity)
    sent_order = sent_order.reshape(feat_count, clus_count, capacity)
    arrived = (
        lax.all_to_all(
            lax.all_to_all(sent, "feat", split_axis=0, concat_axis=0, tiled=True),
            "clus",
            split_axis=1,
            concat_axis=1,
            tiled=True,
        ),
        lax.all_to_all(
            lax.all_to_all(sent_cluster, "feat", split_axis=0, concat_axis=0, tiled=True),
            "clus",
            split_axis=1,
            concat_axis=1,
            tiled=True,
        ),
        lax.all_to_all(
            lax.all_to_all(sent_order, "feat", split_axis=0, concat_axis=0, tiled=True),
            "clus",
            split_axis=1,
            concat_axis=1,
            tiled=True,
        ),
    )
    keys = arrived[0].reshape(owners * capacity, keep)
    arrived_cluster = arrived[1].reshape(owners * capacity)
    arrived_order = arrived[2].reshape(owners * capacity)
    scores = compare_rows(keys, arrived_cluster, arrived_order)
    scores = scores.reshape(feat_count, clus_count, capacity)
    returned = lax.all_to_all(
        lax.all_to_all(scores, "feat", split_axis=0, concat_axis=0, tiled=True),
        "clus",
        split_axis=1,
        concat_axis=1,
        tiled=True,
    )
    values = returned.reshape(owners * capacity)[slot]
    return values.reshape(1, rows_here)


def solution(mesh):
    return jax.shard_map(
        local,
        mesh=mesh,
        in_specs=(P("clus", "feat"), P("feat"), P(), P("clus"), P("clus")),
        out_specs=P("clus", "feat"),
        check_vma=False,
    )
```

profile of v0, /device:TPU:1, one launch (start us, length us, event | category | flops | bytes accessed | tf_op | source)
XLA Modules:
  0.0 362.0 jit_solution(7280753167751387581)
XLA Ops:
  1.3 3.4 scatter_custom_fusion
  5.7 9.0 %all-to-all-start = ((s32[8,1,384]{2,1,0:T(1,128)}), s32[8,1,384]{2,1,0:T(1,128)S(1)}, u32[]{:S(2)}, u32[]{:S(2)}) async-start(s32[8,1,384]{2,1,0:T(1,128)} %reshape.112), calls=%async_computation | async-start | bytes 24576 | tf_op jit(solution)/shard_map/all_to_all | solution.py:91
  15.4 3.7 %broadcast_multiply_fusion = bf16[6144,256]{1,0:T(8,128)(2,1)} fusion(bf16[6144,256]{1,0:T(8,128)(2,1)} %param.9, bf16[256]{0:T(256)(128)(2,1)S(1)} %add_convert_fusion), kind=kLoop, calls=%fused_computation.20 | loop fusion | flops 1572864 | bytes 6291968 | tf_op jit(solution)/shard_map/mul | solution.py:54
  21.3 4.6 %all-to-all-start.4 = ((bf16[8,768,256]{2,1,0:T(8,128)(2,1)}), bf16[8,768,256]{2,1,0:T(8,128)(2,1)S(1)}, u32[]{:S(2)}, u32[]{:S(2)}) async-start(bf16[8,768,256]{2,1,0:T(8,128)(2,1)} %bitcast.4), calls=%async_computation.4 | async-start | bytes 6291456 | tf_op jit(solution)/shard_map/all_to_all | solution.py:57
  26.7 3.4 scatter_custom_fusion.1
  33.1 67.0 %all-to-all-done.4 = bf16[8,768,256]{2,1,0:T(8,128)(2,1)S(1)} async-done(((bf16[8,768,256]{2,1,0:T(8,128)(2,1)}), bf16[8,768,256]{2,1,0:T(8,128)(2,1)S(1)}, u32[]{:S(2)}, u32[]{:S(2)}) %all-to-all-start.4) | async-done | bytes 3145760 | tf_op jit(solution)/shard_map/all_to_all | solution.py:57
  105.4 7.2 %convolution_bitcast_fusion = f32[768,8,256]{2,1,0:T(8,128)} fusion(f32[768,8,256]{2,1,0:T(8,128)S(1)} %fusion.3, f32[8,8,1]{0,1,2:T(8,128)S(1)} %copy-done.8), kind=kOutput, calls=%fused_computation.15 | convolution fusion | flops 150994944 | bytes 12583168 | tf_op jit(solution)/shard_map/rab,ad->rdb/dot_general | solution.py:61
  112.7 6.6 %copy.66 = f32[768,8,256]{0,2,1:T(8,128)} copy(f32[768,8,256]{2,1,0:T(8,128)} %convolution_bitcast_fusion) | data formatting | bytes 12582912 | tf_op jit(solution)/shard_map/reshape | solution.py:63
  119.3 5.3 %gather_fusion = f32[512,768]{1,0:T(8,128)S(1)} fusion(f32[768,2048]{0,1:T(8,128)} %bitcast.42, s32[1024]{0:T(1024)S(1)} %pad_clamp_fusion.1), kind=kCustom, calls=%fused_computation | custom fusion | bytes 3147776 | tf_op jit(solution)/shard_map/jit(_take)/gather | solution.py:64
  124.8 7.7 %all-to-all-start.1 = ((s32[8,32,12]{2,0,1:T(8,128)}), s32[8,32,12]{2,0,1:T(8,128)S(1)}, u32[]{:S(2)}, u32[]{:S(2)}) async-start(s32[8,32,12]{2,0,1:T(8,128)} %copy.49), calls=%async_computation.1 | async-start | bytes 262144 | tf_op jit(solution)/shard_map/all_to_all | solution.py:90
  133.9 7.1 %scatter_custom_fusion.2 = bf16[3072,512]{1,0:T(8,128)(2,1)S(1)} fusion(s32[768]{0:T(1024)S(1)} %compare_select_fusion, bf16[768,512]{1,0:T(8,128)(2,1)} %copy.56, bf16[]{:T(256)} %constant.38.clone.1), kind=kCustom, calls=%fused_computation.21 | custom fusion | bytes 3146240 | tf_op jit(solution)/shard_map/scatter | solution.py:76
  143.7 5.8 %copy.57 = bf16[8,32,12,512]{3,1,2,0:T(8,128)(2,1)} copy(bf16[8,32,12,512]{3,2,1,0:T(8,128)(2,1)} %reshape.55) | data formatting | bytes 6291456 | tf_op jit(solution)/shard_map/reshape | solution.py:79
  149.5 6.8 %all-to-all-start.5 = ((bf16[8,32,12,512]{3,1,2,0:T(8,128)(2,1)}), bf16[8,32,12,512]{3,1,2,0:T(8,128)(2,1)S(1)}, u32[]{:S(2)}, u32[]{:S(2)}) async-start(bf16[8,32,12,512]{3,1,2,0:T(8,128)(2,1)} %copy.57), calls=%async_computation.5 | async-start | bytes 6291456 | tf_op jit(solution)/shard_map/all_to_all | solution.py:84
  157.9 72.7 %all-to-all-done.5 = bf16[8,32,12,512]{3,1,2,0:T(8,128)(2,1)S(1)} async-done(((bf16[8,32,12,512]{3,1,2,0:T(8,128)(2,1)}), bf16[8,32,12,512]{3,1,2,0:T(8,128)(2,1)S(1)}, u32[]{:S(2)}, u32[]{:S(2)}) %all-to-all-start.5) | async-done | bytes 3145760 | tf_op jit(solution)/shard_map/all_to_all | solution.py:84
  230.6 7.5 %all-to-all-start.3 = ((s32[8,32,12]{2,0,1:T(8,128)}), s32[8,32,12]{2,0,1:T(8,128)S(1)}, u32[]{:S(2)}, u32[]{:S(2)}) async-start(s32[8,32,12]{2,0,1:T(8,128)} %copy.52), calls=%async_computation.3 | async-start | bytes 262144 | tf_op jit(solution)/shard_map/all_to_all | solution.py:97
  238.1 3.4 copy.58
  241.5 4.2 %all-to-all-done.3 = s32[8,32,12]{2,0,1:T(8,128)S(1)} async-done(((s32[8,32,12]{2,0,1:T(8,128)}), s32[8,32,12]{2,0,1:T(8,128)S(1)}, u32[]{:S(2)}, u32[]{:S(2)}) %all-to-all-start.3) | async-done | bytes 12320 | tf_op jit(solution)/shard_map/all_to_all | solution.py:97
  245.7 4.1 %all-to-all-start.6 = ((bf16[8,32,12,512]{3,0,2,1:T(8,128)(2,1)}), bf16[8,32,12,512]{3,0,2,1:T(8,128)(2,1)S(1)}, u32[]{:S(2)}, u32[]{:S(2)}) async-start(bf16[8,32,12,512]{3,0,2,1:T(8,128)(2,1)} %copy.58), calls=%async_computation.6 | async-start | bytes 6291456 | tf_op jit(solution)/shard_map/all_to_all | solution.py:83
  251.1 38.0 %all-to-all-done.6 = bf16[8,32,12,512]{3,0,2,1:T(8,128)(2,1)S(1)} async-done(((bf16[8,32,12,512]{3,0,2,1:T(8,128)(2,1)}), bf16[8,32,12,512]{3,0,2,1:T(8,128)(2,1)S(1)}, u32[]{:S(2)}, u32[]{:S(2)}) %all-to-all-start.6) | async-done | bytes 3145760 | tf_op jit(solution)/shard_map/all_to_all | solution.py:83
  292.2 4.8 %reshape_reshape.14 = bf16[6,512,512]{2,1,0:T(8,128)(2,1)S(1)} reshape(bf16[8,32,12,512]{3,2,1,0:T(8,128)(2,1)} %copy.59) | data formatting | bytes 6291456 | tf_op jit(solution)/shard_map/reshape;reshape | solution.py:37
  297.0 6.2 %reshape.56 = bf16[3072,512]{1,0:T(8,128)(2,1)} reshape(bf16[8,32,12,512]{3,2,1,0:T(8,128)(2,1)} %copy.59) | data formatting | bytes 6291456 | tf_op jit(solution)/shard_map/reshape | solution.py:105
  303.3 26.8 %while.11 = (s32[]{:T(128)}, f32[6,512]{1,0:T(8,128)S(1)}, s32[8,32,12]{2,1,0:T(8,128)}, s32[6,512]{1,0:T(8,128)S(1)}, s32[8,32,12]{2,1,0:T(8,128)}, /*index=5*/...) while((s32[]{:T(128)}, f32[6,512]{1,0:T(8,128)S(1)}, ...), condition=%wide.wide.region_7.8_spmd, body=%wide.wide.region_5.7_spmd.sunk | while | flops 1620052480 | bytes 3731593 | solution.py:41
  303.3 4.4 %select_reduce_fusion.3 = f32[512]{0:T(512)S(1)} fusion(bf16[3072,512]{1,0:T(8,128)(2,1)} %get-tuple-element.221, s32[3072]{0:T(1024)S(1)} %get-tuple-element.222, s32[3072]{0:T(1024)S(1)} %get-tuple-element.223, s32[512]{0:T(512)S(1)} %bitcast.49, s32[512]{0:T(512)S(1)} %bitcast.50, pred[3072]{0:T(1024)(128)(4,1)S(1)} %broadcast_compare_fusion.3, ...), kind=kOutput, calls=%fused_computation.5.clone.clone.1 | convolution fusion | flops 1620049408 | bytes 3703812 | tf_op jit(solution)/shard_map/while/body/eval_jaxpr/dot_general | solution.py:26
  307.8 4.4 %select_reduce_fusion.3 = f32[512]{0:T(512)S(1)} fusion(bf16[3072,512]{1,0:T(8,128)(2,1)} %get-tuple-element.221, s32[3072]{0:T(1024)S(1)} %get-tuple-element.222, s32[3072]{0:T(1024)S(1)} %get-tuple-element.223, s32[512]{0:T(512)S(1)} %bitcast.49, s32[512]{0:T(512)S(1)} %bitcast.50, pred[3072]{0:T(1024)(128)(4,1)S(1)} %broadcast_compare_fusion.3, ...), kind=kOutput, calls=%fused_computation.5.clone.clone.1 | convolution fusion | flops 1620049408 | bytes 3703812 | tf_op jit(solution)/shard_map/while/body/eval_jaxpr/dot_general | solution.py:26
  312.2 4.3 %select_reduce_fusion.3 = f32[512]{0:T(512)S(1)} fusion(bf16[3072,512]{1,0:T(8,128)(2,1)} %get-tuple-element.221, s32[3072]{0:T(1024)S(1)} %get-tuple-element.222, s32[3072]{0:T(1024)S(1)} %get-tuple-element.223, s32[512]{0:T(512)S(1)} %bitcast.49, s32[512]{0:T(512)S(1)} %bitcast.50, pred[3072]{0:T(1024)(128)(4,1)S(1)} %broadcast_compare_fusion.3, ...), kind=kOutput, calls=%fused_computation.5.clone.clone.1 | convolution fusion | flops 1620049408 | bytes 3703812 | tf_op jit(solution)/shard_map/while/body/eval_jaxpr/dot_general | solution.py:26
  316.7 4.3 %select_reduce_fusion.3 = f32[512]{0:T(512)S(1)} fusion(bf16[3072,512]{1,0:T(8,128)(2,1)} %get-tuple-element.221, s32[3072]{0:T(1024)S(1)} %get-tuple-element.222, s32[3072]{0:T(1024)S(1)} %get-tuple-element.223, s32[512]{0:T(512)S(1)} %bitcast.49, s32[512]{0:T(512)S(1)} %bitcast.50, pred[3072]{0:T(1024)(128)(4,1)S(1)} %broadcast_compare_fusion.3, ...), kind=kOutput, calls=%fused_computation.5.clone.clone.1 | convolution fusion | flops 1620049408 | bytes 3703812 | tf_op jit(solution)/shard_map/while/body/eval_jaxpr/dot_general | solution.py:26
  321.2 4.3 %select_reduce_fusion.3 = f32[512]{0:T(512)S(1)} fusion(bf16[3072,512]{1,0:T(8,128)(2,1)} %get-tuple-element.221, s32[3072]{0:T(1024)S(1)} %get-tuple-element.222, s32[3072]{0:T(1024)S(1)} %get-tuple-element.223, s32[512]{0:T(512)S(1)} %bitcast.49, s32[512]{0:T(512)S(1)} %bitcast.50, pred[3072]{0:T(1024)(128)(4,1)S(1)} %broadcast_compare_fusion.3, ...), kind=kOutput, calls=%fused_computation.5.clone.clone.1 | convolution fusion | flops 1620049408 | bytes 3703812 | tf_op jit(solution)/shard_map/while/body/eval_jaxpr/dot_general | solution.py:26
  325.6 4.3 %select_reduce_fusion.3 = f32[512]{0:T(512)S(1)} fusion(bf16[3072,512]{1,0:T(8,128)(2,1)} %get-tuple-element.221, s32[3072]{0:T(1024)S(1)} %get-tuple-element.222, s32[3072]{0:T(1024)S(1)} %get-tuple-element.223, s32[512]{0:T(512)S(1)} %bitcast.49, s32[512]{0:T(512)S(1)} %bitcast.50, pred[3072]{0:T(1024)(128)(4,1)S(1)} %broadcast_compare_fusion.3, ...), kind=kOutput, calls=%fused_computation.5.clone.clone.1 | convolution fusion | flops 1620049408 | bytes 3703812 | tf_op jit(solution)/shard_map/while/body/eval_jaxpr/dot_general | solution.py:26
  330.4 9.0 %all_to_all.56 = f32[8,1,384]{2,1,0:T(1,128)S(1)} all-to-all(f32[8,1,384]{2,1,0:T(1,128)S(1)} %reshape.116), channel_id=1, replica_groups=mesh['feat'=8,'clus'=32] {'feat'}, dimensions={0} | all-to-all | bytes 24576 | tf_op jit(solution)/shard_map/all_to_all | solution.py:111
  341.4 7.7 %all-to-all-start.8 = ((f32[8,32,12]{2,0,1:T(8,128)}), f32[8,32,12]{2,0,1:T(8,128)S(1)}, u32[]{:S(2)}, u32[]{:S(2)}) async-start(f32[8,32,12]{2,0,1:T(8,128)} %copy.64), calls=%async_computation.8 | async-start | bytes 262144 | tf_op jit(solution)/shard_map/all_to_all | solution.py:110
  349.1 7.7 %all-to-all-done.8 = f32[8,32,12]{2,0,1:T(8,128)S(1)} async-done(((f32[8,32,12]{2,0,1:T(8,128)}), f32[8,32,12]{2,0,1:T(8,128)S(1)}, u32[]{:S(2)}, u32[]{:S(2)}) %all-to-all-start.8) | async-done | bytes 12320 | tf_op jit(solution)/shard_map/all_to_all | solution.py:110
  357.0 4.5 %gather_fusion.1 = f32[768]{0:T(1024)S(1)} fusion(f32[3072]{0:T(1024)S(1)} %reshape.57, s32[1024]{0:T(1024)S(1)} %pad_clamp_fusion), kind=kCustom, calls=%fused_computation.1 | custom fusion | bytes 9216 | tf_op jit(solution)/shard_map/gather | solution.py:117
  (86 shorter events, 27.9 us)
Async XLA Ops:
  1.3 132.6 %copy-start.4 = (s32[768]{0:T(1024)}, s32[768]{0:T(1024)S(1)}, u32[]{:S(2)}) copy-start(s32[768]{0:T(1024)S(1)} %compare_select_fusion) | copy-start | bytes 9220
  5.7 15.6 %all-to-all-start = ((s32[8,1,384]{2,1,0:T(1,128)}), s32[8,1,384]{2,1,0:T(1,128)S(1)}, u32[]{:S(2)}, u32[]{:S(2)}) async-start(s32[8,1,384]{2,1,0:T(1,128)} %reshape.112), calls=%async_computation | async-start | bytes 24576 | tf_op jit(solution)/shard_map/all_to_all | solution.py:91
  21.3 9.7 %copy-start.7 = (s32[512]{0:T(512)S(1)}, s32[512]{0:T(512)}, u32[]{:S(2)}) copy-start(s32[512]{0:T(512)} %param.11) | copy-start | bytes 6148
  21.3 82.2 %copy-start.2 = (bf16[256,256,1]{1,0,2:T(8,128)(2,1)S(1)}, bf16[256,256,1]{1,0,2:T(8,128)(2,1)}, u32[]{:S(2)}) copy-start(bf16[256,256,1]{1,0,2:T(8,128)(2,1)} %constant.83) | copy-start | bytes 393220
  21.3 78.8 %all-to-all-start.4 = ((bf16[8,768,256]{2,1,0:T(8,128)(2,1)}), bf16[8,768,256]{2,1,0:T(8,128)(2,1)S(1)}, u32[]{:S(2)}, u32[]{:S(2)}) async-start(bf16[8,768,256]{2,1,0:T(8,128)(2,1)} %bitcast.4), calls=%async_computation.4 | async-start | bytes 6291456 | tf_op jit(solution)/shard_map/all_to_all | solution.py:57
  100.1 24.7 %all-to-all-start.2 = ((s32[8,1,384]{2,1,0:T(1,128)}), s32[8,1,384]{2,1,0:T(1,128)S(1)}, u32[]{:S(2)}, u32[]{:S(2)}) async-start(s32[8,1,384]{2,1,0:T(1,128)} %reshape.114), calls=%async_computation.2 | async-start | bytes 24576 | tf_op jit(solution)/shard_map/all_to_all | solution.py:98
  103.5 1.9 copy-start.8
  124.8 24.7 %all-to-all-start.1 = ((s32[8,32,12]{2,0,1:T(8,128)}), s32[8,32,12]{2,0,1:T(8,128)S(1)}, u32[]{:S(2)}, u32[]{:S(2)}) async-start(s32[8,32,12]{2,0,1:T(8,128)} %copy.49), calls=%async_computation.1 | async-start | bytes 262144 | tf_op jit(solution)/shard_map/all_to_all | solution.py:90
  149.5 81.1 %all-to-all-start.5 = ((bf16[8,32,12,512]{3,1,2,0:T(8,128)(2,1)}), bf16[8,32,12,512]{3,1,2,0:T(8,128)(2,1)S(1)}, u32[]{:S(2)}, u32[]{:S(2)}) async-start(bf16[8,32,12,512]{3,1,2,0:T(8,128)(2,1)} %copy.57), calls=%async_computation.5 | async-start | bytes 6291456 | tf_op jit(solution)/shard_map/all_to_all | solution.py:84
  230.6 15.2 %all-to-all-start.3 = ((s32[8,32,12]{2,0,1:T(8,128)}), s32[8,32,12]{2,0,1:T(8,128)S(1)}, u32[]{:S(2)}, u32[]{:S(2)}) async-start(s32[8,32,12]{2,0,1:T(8,128)} %copy.52), calls=%async_computation.3 | async-start | bytes 262144 | tf_op jit(solution)/shard_map/all_to_all | solution.py:97
  245.7 43.3 %all-to-all-start.6 = ((bf16[8,32,12,512]{3,0,2,1:T(8,128)(2,1)}), bf16[8,32,12,512]{3,0,2,1:T(8,128)(2,1)S(1)}, u32[]{:S(2)}, u32[]{:S(2)}) async-start(bf16[8,32,12,512]{3,0,2,1:T(8,128)(2,1)} %copy.58), calls=%async_computation.6 | async-start | bytes 6291456 | tf_op jit(solution)/shard_map/all_to_all | solution.py:83
  249.9 42.3 %copy-start = (s32[8,32,12]{2,1,0:T(8,128)}, s32[8,32,12]{2,1,0:T(8,128)S(1)}, u32[]{:S(2)}) copy-start(s32[8,32,12]{2,1,0:T(8,128)S(1)} %copy.62) | copy-start | bytes 36868
  250.8 41.4 %copy-start.1 = (s32[8,32,12]{2,1,0:T(8,128)}, s32[8,32,12]{2,1,0:T(8,128)S(1)}, u32[]{:S(2)}) copy-start(s32[8,32,12]{2,1,0:T(8,128)S(1)} %copy.61) | copy-start | bytes 36868
  297.0 6.3 %copy-start.3 = (f32[6,512]{1,0:T(8,128)S(1)}, f32[6,512]{1,0:T(8,128)}, u32[]{:S(2)}) copy-start(f32[6,512]{1,0:T(8,128)} %custom-call.4) | copy-start | bytes 36868
  297.0 6.3 %copy-start.6 = (s32[3072]{0:T(1024)S(1)}, s32[3072]{0:T(1024)}, u32[]{:S(2)}) copy-start(s32[3072]{0:T(1024)} %lt.53) | copy-start | bytes 36868
  303.3 45.9 %copy-start.5 = (s32[768]{0:T(1024)S(1)}, s32[768]{0:T(1024)}, u32[]{:S(2)}) copy-start(s32[768]{0:T(1024)} %copy-done.4) | copy-start | bytes 9220
  341.4 15.4 %all-to-all-start.8 = ((f32[8,32,12]{2,0,1:T(8,128)}), f32[8,32,12]{2,0,1:T(8,128)S(1)}, u32[]{:S(2)}, u32[]{:S(2)}) async-start(f32[8,32,12]{2,0,1:T(8,128)} %copy.64), calls=%async_computation.8 | async-start | bytes 262144 | tf_op jit(solution)/shard_map/all_to_all | solution.py:110
where the time goes:
time: 363 us; the launch traced here: 362 us
  waiting for transfers between devices  192 us (53%)
  local copies, waits for them, and re-layouts  66.4 us (18%)
  starting transfers between devices  50.8 us (14%)
  matrix products  35.8 us (10%)
  blocking collectives  8.96 us (2%)
  other arithmetic  7.75 us (2%)
    all_to_all x1, waiting for transfers between devices, local(): lax.all_to_all(sent, 'feat', split_axis=0, concat_axis=0, tiled=True)  72.7 us
    all_to_all x1, waiting for transfers between devices, local(): lax.all_to_all(signed, 'feat', split_axis=0, concat_axis=1, tiled=True)  67 us
    all_to_all x1, waiting for transfers between devices, local(): lax.all_to_all(lax.all_to_all(sent, 'feat', split_axis=0, concat_axis=0,...  38 us
    dot_general x6, matrix products, one_block(): lax.dot_general(queries, keys, (((1,), (1,)), ((), ())), preferred_elemen...  26.1 us
    all_to_all x1, starting transfers between devices, local(): lax.all_to_all(sent_cluster, 'feat', split_axis=0, concat_axis=0, tiled=T...  9.01 us
    all_to_all x1, blocking collectives, local(): lax.all_to_all(scores, 'feat', split_axis=0, concat_axis=0, tiled=True)  8.96 us
    reshape x2, local copies, waits for them, and re-layouts, local(): sent = sent.reshape(feat_count, clus_count, capacity, keep)  8.43 us
    all_to_all x1, waiting for transfers between devices, local(): lax.all_to_all(lax.all_to_all(scores, 'feat', split_axis=0, concat_axis=0...  7.72 us
  transfers between devices with their start and end apart: 8, of which 6 were waited for; matrix products, arithmetic and copies ran while one was open for 15% of the time, Pallas kernels for 0%

commit v1 on v0

--- a/solution.py
+++ b/solution.py
@@ -1,7 +1,11 @@
+import functools
+
 import jax
 import jax.numpy as jnp
 import numpy as np
 from jax import lax
+from jax.experimental import pallas as pl
+from jax.experimental.pallas import tpu as pltpu
 from jax.sharding import PartitionSpec as P
 
 CL_OWN = 16
@@ -41,7 +45,7 @@
     return lax.map(one_block, parts_in).reshape(total)
 
 
-def local(embeddings, signs, coords, cluster, order):
+def general(embeddings, signs, coords, cluster, order):
     feat_count = lax.axis_size("feat")
     clus_count = lax.axis_size("clus")
     owners = feat_count * clus_count
@@ -118,6 +122,449 @@
     return values.reshape(1, rows_here)
 
 
+LIVE = 5
+RELAY = 6
+PLACES = 32
+DEVS = LIVE * PLACES
+HALVES = 2
+SLOTS = 720
+TILE = 144
+ROOM = 80
+KEEP = 512
+WIDTH = 256
+GROUP = 6144
+HALF = GROUP // HALVES
+HERE = 768
+COMPACT = HALVES * SLOTS
+RECORDS = PLACES * ROOM
+STRIDE = 4096
+ORDER_BITS = 18
+BATCH = 4
+MESH_ID = pl.DeviceIdType.MESH
+RELAYED = ((0, 3), (0, 4), (1, 4), (3, 0), (4, 0), (4, 1))
+RELAY_ORDER = (1, 4, 2, 3, 0, 5)
+BF = jnp.bfloat16
+F32 = jnp.float32
+I32 = jnp.int32
+NT = (((1,), (1,)), ((), ()))
+
+
+def iota(shape, dim):
+    return lax.broadcasted_iota(I32, shape, dim)
+
+
+def pick(mask):
+    return jnp.where(mask, jnp.float32(1), jnp.float32(0)).astype(BF)
+
+
+def dot(a, b):
+    return jnp.dot(a, b, preferred_element_type=F32)
+
+
+def dot_nt(a, b):
+    return lax.dot_general(a, b, NT, preferred_element_type=F32)
+
+
+def fast_kernel(
+    x_ref, signs_ref, coords_ref, cluster_ref, order_ref,
+    out_ref, flag_ref,
+    key_ref, dev_ref, rank_ref, meta_ref, cm_ref, had_ref,
+    sb_ref, rb_ref, relay_ref, unit_ref, s2_ref, r2_ref, sm_ref, rm_ref,
+    best_ref, rs_ref, rr_ref, tg_ref,
+    zs_sem, zr_sem, ys_sem, yr_sem, us_sem, ur_sem, ms_sem, mr_sem, bs_sem, br_sem, ts_sem, tr_sem, own_sem,
+):
+    z = lax.axis_index("feat")
+    c = lax.axis_index("clus")
+    live = z < LIVE
+    barrier = pltpu.get_barrier_semaphore()
+    for s in range(LIVE):
+        @pl.when(z != s)
+        def _():
+            pl.semaphore_signal(barrier, inc=1, device_id={"feat": s}, device_id_type=MESH_ID)
+
+    @pl.when((z == 0) | (z == 1) | (z == 3) | (z == 4))
+    def _():
+        pl.semaphore_signal(barrier, inc=1, device_id={"feat": RELAY}, device_id_type=MESH_ID)
+
+    @pl.when(live)
+    def _():
+        def greet(i, carry):
+            pl.semaphore_signal(barrier, inc=1, device_id={"clus": lax.rem(c + i, PLACES)}, device_id_type=MESH_ID)
+            return carry
+        lax.fori_loop(1, PLACES, greet, 0)
+
+    meta_ref[...] = jnp.zeros_like(meta_ref)
+    upper = pick(iota((WIDTH, WIDTH + 128), 0) < jnp.where(iota((WIDTH, WIDTH + 128), 1) < WIDTH, iota((WIDTH, WIDTH + 128), 1), WIDTH))
+    classes = DEVS + 8
+
+    def rank_block(b, base):
+        at = pl.ds(pl.multiple_of(b * WIDTH, WIDTH), WIDTH)
+        cl = cluster_ref[0:1, at]
+        place = order_ref[0:1, at]
+        spread = (cl >> 4) + 63 * (cl & 15)
+        dev = spread - DEVS * ((spread.astype(F32) + 0.5) * (1.0 / DEVS)).astype(I32)
+        q = ((dev.astype(F32) + 0.5) * (1.0 / LIVE)).astype(I32)
+        plane = dev - LIVE * q
+        line = iota((classes, WIDTH), 0)
+        member = jnp.where((line == dev) | (line == plane + DEVS), jnp.float32(1), jnp.float32(0))
+        counts = dot(member.astype(BF), upper)
+        before = member * (counts[:, :WIDTH] + jnp.concatenate([base, base], axis=1))
+        rank = jnp.sum(before[:DEVS], axis=0, keepdims=True).astype(I32)
+        slot = jnp.sum(before[DEVS:], axis=0, keepdims=True).astype(I32)
+        key_ref[0:1, at] = plane * STRIDE + slot
+        dev_ref[0:1, at] = plane * PLACES + q
+        rank_ref[0:1, at] = rank
+        key = (cl << ORDER_BITS) + place
+        row = iota((16, WIDTH), 0)
+        info = jnp.where(row == 0, key & 255, 0)
+        info = jnp.where(row == 1, (key >> 8) & 255, info)
+        info = jnp.where(row == 2, (key >> 16) & 255, info)
+        info = jnp.where(row == 3, (key >> 24) & 255, info)
+        info = jnp.where(row == 4, 1, info)
+        info = jnp.where(row == 5, q, info)
+        info = jnp.where(row == 6, rank, info)
+        meta_ref[0:16, at] = info.astype(F32).astype(BF)
+        return base + counts[:, WIDTH:]
+
+    base = jnp.zeros((classes, 128), F32)
+    most = jnp.zeros((8, 128), F32)
+    per_half = HALF // WIDTH
+    for h in range(HALVES):
+        base = lax.fori_loop(h * per_half, (h + 1) * per_half, rank_block, base)
+        most = jnp.maximum(most, base[DEVS:])
+        base = jnp.concatenate([base[:DEVS], jnp.zeros((8, 128), F32)], axis=0)
+    over = jnp.where(jnp.max(most) > SLOTS, jnp.float32(1), jnp.float32(0))
+    over = jnp.maximum(over, jnp.where(jnp.max(base[:DEVS]) > ROOM, jnp.float32(1), jnp.float32(0)))
+
+    @pl.when(live)
+    def _():
+        pl.semaphore_wait(barrier, 7 + PLACES - 1)
+
+    @pl.when(z == RELAY)
+    def _():
+        pl.semaphore_wait(barrier, 4)
+
+    def target(i):
+        down = 4 - i
+        down = jnp.where(down <= z, down - 1, down)
+        up = jnp.where(i >= z, i + 1, i)
+        return jnp.where(z < 2, down, up)
+
+    def far(p):
+        return (p - z >= 3) | (z - p >= 3)
+
+    def relay_slot(p):
+        return jnp.where(p > z, z + p - 3, z + p)
+
+    def direct_copy(i, h, p):
+        return pltpu.make_async_remote_copy(
+            src_ref=sb_ref.at[i, h], dst_ref=rb_ref.at[h, z],
+            send_sem=zs_sem.at[i, h], recv_sem=zr_sem.at[h, z],
+            device_id={"feat": p}, device_id_type=MESH_ID)
+
+    def relay_copy(i, h, p):
+        slot = relay_slot(p)
+        return pltpu.make_async_remote_copy(
+            src_ref=sb_ref.at[i, h], dst_ref=relay_ref.at[slot, h],
+            send_sem=zs_sem.at[i, h], recv_sem=yr_sem.at[slot, h],
+            device_id={"feat": RELAY}, device_id_type=MESH_ID)
+
+    def forward_copy(r, h):
+        src, dst = RELAYED[r]
+        return pltpu.make_async_remote_copy(
+            src_ref=relay_ref.at[r, h], dst_ref=rb_ref.at[h, src],
+            send_sem=ys_sem.at[r, h], recv_sem=zr_sem.at[h, src],
+            device_id={"feat": dst}, device_id_type=MESH_ID)
+
+    def unit_copy(q):
+        return pltpu.make_async_remote_copy(
+            src_ref=s2_ref.at[q], dst_ref=r2_ref.at[c],
+            send_sem=us_sem.at[q], recv_sem=ur_sem.at[c],
+            device_id={"clus": q}, device_id_type=MESH_ID)
+
+    def meta_copy(q):
+        return pltpu.make_async_remote_copy(
+            src_ref=sm_ref.at[q], dst_ref=rm_ref.at[c],
+            send_sem=ms_sem.at[q], recv_sem=mr_sem.at[c],
+            device_id={"clus": q}, device_id_type=MESH_ID)
+
+    def best_copy(q):
+        return pltpu.make_async_remote_copy(
+            src_ref=rs_ref.at[q], dst_ref=rr_ref.at[c],
+            send_sem=bs_sem.at[q], recv_sem=br_sem.at[c],
+            device_id={"clus": q}, device_id_type=MESH_ID)
+
+    def table_copy(p):
+        return pltpu.make_async_remote_copy(
+            src_ref=tg_ref.at[z], dst_ref=tg_ref.at[z],
+            send_sem=ts_sem.at[p], recv_sem=tr_sem.at[z],
+            device_id={"feat": p}, device_id_type=MESH_ID)
+
+    def arrival(ref, sem, index):
+        return pltpu.make_async_copy(ref.at[index], ref.at[index], sem.at[index])
+
+    @pl.when(live)
+    def _():
+        sign = (2 * signs_ref[...] - 1).astype(F32)
+
+        def chosen(h, p, t):
+            keys = key_ref[0:1, h * HALF:(h + 1) * HALF]
+            return pick(keys == iota((TILE, HALF), 0) + (p * STRIDE + t * TILE))
+
+        for h in range(HALVES):
+            def send_chunk(i, carry, h=h):
+                p = target(i)
+
+                def tile(t, carry):
+                    rows = dot(chosen(h, p, t), x_ref[h * HALF:(h + 1) * HALF, :])
+                    sb_ref[i, h, pl.ds(pl.multiple_of(t * TILE, TILE), TILE), :] = (rows * sign).astype(BF)
+                    return carry
+                lax.fori_loop(0, SLOTS // TILE, tile, 0)
+
+                @pl.when(far(p))
+                def _():
+                    relay_copy(i, h, p).start()
+
+                @pl.when(jnp.logical_not(far(p)))
+                def _():
+                    direct_copy(i, h, p).start()
+                return carry
+            lax.fori_loop(0, LIVE - 1, send_chunk, 0)
+
+        for h in range(HALVES):
+            def own(t, carry, h=h):
+                at = pl.ds(pl.multiple_of(t * TILE, TILE), TILE)
+                hot = chosen(h, z, t)
+                rows = dot(hot, x_ref[h * HALF:(h + 1) * HALF, :])
+                rb_ref[h, z, at, :] = (rows * sign).astype(BF)
+                info = dot_nt(hot, meta_ref[:, h * HALF:(h + 1) * HALF])
+                cm_ref[pl.ds(pl.multiple_of(h * SLOTS + t * TILE, TILE), TILE), :] = info.astype(BF)
+                return carry
+            lax.fori_loop(0, SLOTS // TILE, own, 0)
+
+        unit16 = pick(iota((16, 128), 0) == iota((16, 128), 1))
+        lanes = dot_nt(unit16, cm_ref[...])
+        goal = jnp.where(lanes[4:5] > 0.5, lanes[5:6] * ROOM + lanes[6:7], -1.0).astype(I32)
+
+        def placed(g):
+            return pick(goal == iota((BATCH * ROOM, COMPACT), 0) + g * (BATCH * ROOM))
+
+        def batch_of(i):
+            return lax.rem(lax.div(c, BATCH) + 1 + i, PLACES // BATCH)
+
+        def send_all(copy, g, source, sink, sem):
+            def one(k, carry):
+                q = g * BATCH + k
+
+                @pl.when(q != c)
+                def _():
+                    copy(q).start()
+
+                @pl.when(q == c)
+                def _():
+                    own_copy = pltpu.make_async_copy(source.at[q], sink.at[q], sem)
+                    own_copy.start()
+                    own_copy.wait()
+                return carry
+            lax.fori_loop(0, BATCH, one, 0)
+
+        def send_meta(i, carry):
+            g = batch_of(i)
+            info = dot(placed(g), cm_ref[...])
+            info = jnp.where(iota(info.shape, 1) == 5, over, info)
+            sm_ref[pl.ds(g * BATCH, BATCH)] = info.astype(BF).reshape(BATCH, ROOM, 128)
+            send_all(meta_copy, g, sm_ref, rm_ref, own_sem)
+            return carry
+        lax.fori_loop(0, PLACES // BATCH, send_meta, 0)
+
+        def walsh(t, carry):
+            at = pl.ds(pl.multiple_of(t * 128, 128), 128)
+            both = (iota((128, KEEP), 0) + t * 128) & coords_ref[...]
+            both = both ^ (both >> 8)
+            both = both ^ (both >> 4)
+            both = both ^ (both >> 2)
+            both = both ^ (both >> 1)
+            had_ref[at, :] = (1 - 2 * (both & 1)).astype(F32).astype(BF)
+            return carry
+        lax.fori_loop(0, LIVE * WIDTH // 128, walsh, 0)
+
+        for h in range(HALVES):
+            for s in range(LIVE):
+                @pl.when(z != s)
+                def _():
+                    pltpu.make_async_copy(rb_ref.at[h, s], rb_ref.at[h, s], zr_sem.at[h, s]).wait()
+
+            def transform(t, carry, h=h):
+                at = pl.ds(pl.multiple_of(t * TILE, TILE), TILE)
+                block = jnp.concatenate([rb_ref[h, s, at, :] for s in range(LIVE)], axis=1)
+                sketch = dot(block, had_ref[...])
+                total = jnp.sum(sketch * sketch, axis=1, keepdims=True)
+                unit = sketch * lax.rsqrt(total + 1e-06)
+                unit_ref[pl.ds(pl.multiple_of(h * SLOTS + t * TILE, TILE), TILE), :] = unit.astype(BF)
+                return carry
+            lax.fori_loop(0, SLOTS // TILE, transform, 0)
+
+        def send_unit(i, carry):
+            g = batch_of(i)
+            rows = dot(placed(g), unit_ref[...])
+            s2_ref[pl.ds(g * BATCH, BATCH)] = rows.astype(BF).reshape(BATCH, ROOM, KEEP)
+            send_all(unit_copy, g, s2_ref, r2_ref, own_sem)
+            return carry
+        lax.fori_loop(0, PLACES // BATCH, send_unit, 0)
+
+        def others(action):
+            def one(i, carry):
+                action(lax.rem(c + i, PLACES))
+                return carry
+            lax.fori_loop(1, PLACES, one, 0)
+
+        others(lambda q: arrival(rm_ref, mr_sem, q).wait())
+        others(lambda q: arrival(r2_ref, ur_sem, q).wait())
+
+        lanes = dot_nt(unit16, rm_ref[...].reshape(RECORDS, 128))
+        low = (lanes[0:1] + 256.0 * lanes[1:2] + 65536.0 * lanes[2:3]).astype(I32)
+        query_key = low + (lanes[3:4].astype(I32) << 24)
+        query_low = (query_key >> ORDER_BITS) << ORDER_BITS
+        flag = jnp.max(lanes[5:6])
+        many = 8 * ROOM
+        wide = 512
+        for t in range(RECORDS // wide):
+            mine = query_key[:, t * wide:(t + 1) * wide]
+            floor = query_low[:, t * wide:(t + 1) * wide]
+
+            def compare(k, top, t=t, mine=mine, floor=floor):
+                keys = r2_ref[pl.ds(k * 8, 8)].reshape(many, KEEP)
+                info = rm_ref[pl.ds(k * 8, 8)].reshape(many, 128).astype(F32)
+                key = (info[:, 0:1] + 256.0 * info[:, 1:2] + 65536.0 * info[:, 2:3]).astype(I32)
+                key = key + (info[:, 3:4].astype(I32) << 24)
+                key = jnp.where(info[:, 4:5] > 0.5, key, jnp.int32(2 ** 31 - 1))
+                queries = r2_ref[...].reshape(RECORDS, KEEP)[t * wide:(t + 1) * wide]
+                score = dot_nt(keys, queries)
+                score = jnp.where((key < mine) & (key >= floor), score, 0.0)
+                return jnp.maximum(top, jnp.max(score.reshape(many // 8, 8, wide), axis=0))
+            top = lax.fori_loop(0, PLACES // 8, compare, jnp.zeros((8, wide), F32))
+            best_ref[0:1, t * wide:(t + 1) * wide] = jnp.max(top, axis=0, keepdims=True)
+        best_ref[0:1, RECORDS:] = jnp.zeros((1, 128), F32)
+
+        for q in range(PLACES):
+            start = q * ROOM // 128 * 128
+            window = best_ref[0:1, start:start + 256]
+            window = pltpu.roll(jnp.broadcast_to(window, (8, 256)), (256 - (q * ROOM - start)) % 256, 1)
+            rs_ref[q] = window[:, :128]
+
+        def send_best(q):
+            best_copy(q).start()
+        others(send_best)
+        own_copy = pltpu.make_async_copy(rs_ref.at[c], rr_ref.at[c], own_sem)
+        own_copy.start()
+        own_copy.wait()
+        others(lambda q: arrival(rr_ref, br_sem, q).wait())
+        table = rr_ref[:, 0, :]
+        tg_ref[z] = jnp.where(iota((PLACES, 128), 1) == 127, flag, table)
+        for p in range(8):
+            @pl.when(z != p)
+            def _():
+                table_copy(p).start()
+
+        for h in range(HALVES):
+            def sent(i, carry, h=h):
+                direct_copy(i, h, target(i)).wait_send()
+                return carry
+            lax.fori_loop(0, LIVE - 1, sent, 0)
+        others(lambda q: meta_copy(q).wait_send())
+        others(lambda q: unit_copy(q).wait_send())
+        others(lambda q: best_copy(q).wait_send())
+        for p in range(8):
+            @pl.when(z != p)
+            def _():
+                table_copy(p).wait_send()
+
+    @pl.when(z == RELAY)
+    def _():
+        for h in range(HALVES):
+            for r in RELAY_ORDER:
+                pltpu.make_async_copy(relay_ref.at[r, h], relay_ref.at[r, h], yr_sem.at[r, h]).wait()
+                forward_copy(r, h).start()
+        for h in range(HALVES):
+            for r in RELAY_ORDER:
+                forward_copy(r, h).wait_send()
+
+    for p in range(LIVE):
+        @pl.when(z != p)
+        def _():
+            pltpu.make_async_copy(tg_ref.at[p], tg_ref.at[p], tr_sem.at[p]).wait()
+    table = tg_ref[...].reshape(DEVS, 128)
+    flag_ref[...] = jnp.broadcast_to(jnp.max(jnp.where(iota((DEVS, 128), 1) == 127, table, 0.0)), (1, 128))
+    high = table.astype(BF)
+    left = table - high.astype(F32)
+    middle = left.astype(BF)
+    lowest = (left - middle.astype(F32)).astype(BF)
+    for t in range(HERE // WIDTH):
+        at = pl.ds(pl.multiple_of(z * HERE + t * WIDTH, WIDTH), WIDTH)
+        lane = pick(iota((128, WIDTH), 0) == rank_ref[0:1, at])
+        found = dot(high, lane) + dot(middle, lane) + dot(lowest, lane)
+        found = jnp.where(iota((DEVS, WIDTH), 0) == dev_ref[0:1, at], found, 0.0)
+        out_ref[0:1, t * WIDTH:(t + 1) * WIDTH] = jnp.sum(found, axis=0, keepdims=True)
+
+
+def local(embeddings, signs, coords, cluster, order):
+    vmem = pl.BlockSpec(memory_space=pltpu.VMEM)
+    dma = pltpu.SemaphoreType.DMA
+    best, flag = pl.pallas_call(
+        fast_kernel,
+        out_shape=(jax.ShapeDtypeStruct((1, HERE), F32), jax.ShapeDtypeStruct((1, 128), F32)),
+        in_specs=[vmem] * 5,
+        out_specs=(vmem, vmem),
+        scratch_shapes=[
+            pltpu.VMEM((1, GROUP), I32),
+            pltpu.VMEM((1, GROUP), I32),
+            pltpu.VMEM((1, GROUP), I32),
+            pltpu.VMEM((128, GROUP), BF),
+            pltpu.VMEM((COMPACT, 128), BF),
+            pltpu.VMEM((LIVE * WIDTH, KEEP), BF),
+            pltpu.VMEM((LIVE - 1, HALVES, SLOTS, WIDTH), BF),
+            pltpu.VMEM((HALVES, LIVE, SLOTS, WIDTH), BF),
+            pltpu.VMEM((len(RELAYED), HALVES, SLOTS, WIDTH), BF),
+            pltpu.VMEM((COMPACT, KEEP), BF),
+            pltpu.VMEM((PLACES, ROOM, KEEP), BF),
+            pltpu.VMEM((PLACES, ROOM, KEEP), BF),
+            pltpu.VMEM((PLACES, ROOM, 128), BF),
+            pltpu.VMEM((PLACES, ROOM, 128), BF),
+            pltpu.VMEM((1, RECORDS + 128), F32),
+            pltpu.VMEM((PLACES, 8, 128), F32),
+            pltpu.VMEM((PLACES, 8, 128), F32),
+            pltpu.VMEM((LIVE, PLACES, 128), F32),
+            dma((LIVE - 1, HALVES)),
+            dma((HALVES, LIVE)),
+            dma((len(RELAYED), HALVES)),
+            dma((len(RELAYED), HALVES)),
+            dma((PLACES,)),
+            dma((PLACES,)),
+            dma((PLACES,)),
+            dma((PLACES,)),
+            dma((PLACES,)),
+            dma((PLACES,)),
+            dma((8,)),
+            dma((LIVE,)),
+            dma,
+        ],
+        compiler_params=pltpu.CompilerParams(
+            collective_id=0, has_side_effects=True, vmem_limit_bytes=56 * 1024 * 1024
+        ),
+    )(
+        embeddings,
+        signs.reshape(1, WIDTH),
+        coords.reshape(1, KEEP),
+        cluster.reshape(1, GROUP),
+        order.reshape(1, GROUP),
+    )
+    return lax.cond(
+        flag[0, 0] > 0.5,
+        lambda: general(embeddings, signs, coords, cluster, order),
+        lambda: best,
+    )
+
+
 def solution(mesh):
     return jax.shard_map(
         local,

time: 363 us -> 152 us (0.42)
  waiting for transfers between devices: 192 us -> 0 us
  Pallas kernels: 0 us -> 151 us
  local copies, waits for them, and re-layouts: 66.4 us -> 0.59 us
  starting transfers between devices: 50.8 us -> 0 us
  matrix products: 35.8 us -> 0 us
  blocking collectives: 8.96 us -> 0 us
  other arithmetic: 7.75 us -> 0 us
    all_to_all x8 -> x0, waiting for transfers between devices: 192 us -> none  [the longest x1 72.7 us: local(): lax.all_to_all(sent, 'feat', split_axis=0, concat_axis=0, tiled=True)]
    pallas_call x0 -> x1, Pallas kernels: none -> 151 us  [local(): pl.pallas_call(fast_kernel, out_shape=(jax.ShapeDtypeStruct((1, HERE), F3...]
    all_to_all x8 -> x0, starting transfers between devices: 50.8 us -> none  [the longest x1 9.01 us: local(): lax.all_to_all(sent_cluster, 'feat', split_axis=0, concat_axis=0, tiled=T...]
    dot_general x9 -> x0, matrix products: 35.8 us -> none  [the longest x6 26.1 us: one_block(): lax.dot_general(queries, keys, (((1,), (1,)), ((), ())), preferred_elemen...]
    reshape x10 -> x0, local copies, waits for them, and re-layouts: 22.5 us -> none  [the longest x2 8.43 us: local(): sent = sent.reshape(feat_count, clus_count, capacity, keep)]
    scatter x3 -> x0, local copies, waits for them, and re-layouts: 13.9 us -> none  [the longest x1 7.14 us: local(): sent = jnp.zeros((owners * capacity, keep), jnp.bfloat16).at[slot].set(unit)]
    all_to_all x8 -> x0, local copies, waits for them, and re-layouts: 9.97 us -> none  [the longest x1 3.39 us: local(): lax.all_to_all(sent, 'feat', split_axis=0, concat_axis=0, tiled=True)]
    gather x2 -> x0, local copies, waits for them, and re-layouts: 9.73 us -> none  [the longest x1 5.27 us: local(): sketch = jnp.take(spread, coords, axis=1)]
  transfers between devices with their start and end apart: 8 -> 0, of which waited for: 6 -> 0; matrix products, arithmetic and copies ran while one was open for 15% -> 0% of each run, Pallas kernels for 0% -> 0%
where the time goes in v1:
time: 152 us
  Pallas kernels  151 us (99%)
    pallas_call x1, Pallas kernels, local(): pl.pallas_call(fast_kernel, out_shape=(jax.ShapeDtypeStruct((1, HERE), F3...  151 us

profile of v1, /device:TPU:1, one launch (start us, length us, event | category | flops | bytes accessed | tf_op | source)
XLA Modules:
  0.0 152.2 jit_solution(10458827620134819110)
XLA Ops:
  0.0 0.0 copy-start
  0.0 0.0 copy-start.10
  0.0 0.0 copy-start.4
  0.0 150.7 %shard_map.77 = (f32[1,768]{1,0:T(1,128)S(1)}, f32[1,128]{1,0:T(1,128)}) custom-call(bf16[6144,256]{1,0:T(8,128)(2,1)} %x_ref.1, s32[1,256]{1,0:T(1,128)} %bitcast.62, s32[1,512]{1,0:T(1,128)} %bitcast.61, s32[1,6144]{1,0:T(1,128)} %bitcast.59, s32[1,6144]{1,0:T(1,128)} %bitcast.60), custom_call_target="tpu_custom_call" | custom-call | tf_op jit(solution)/shard_map/pallas_call | solution.py:513
  151.3 0.0 copy-done
  151.3 0.0 copy-done.10
  151.3 0.0 copy-done.4
  151.3 0.2 conditional.1
  151.6 0.6 copy.85
Async XLA Ops:
  0.0 151.3 %copy-start = (bf16[6144,256]{1,0:T(8,128)(2,1)S(1)}, bf16[6144,256]{1,0:T(8,128)(2,1)}, u32[]{:S(2)}) copy-start(bf16[6144,256]{1,0:T(8,128)(2,1)} %x_ref.1) | copy-start | bytes 9437188
  0.0 151.3 %copy-start.10 = (s32[256]{0:T(256)S(1)}, s32[256]{0:T(256)}, u32[]{:S(2)}) copy-start(s32[256]{0:T(256)} %param.12) | copy-start | bytes 3076
  0.0 151.3 %copy-start.4 = (s32[512]{0:T(512)S(1)}, s32[512]{0:T(512)}, u32[]{:S(2)}) copy-start(s32[512]{0:T(512)} %param.13) | copy-start | bytes 6148

commit v2 on v1

--- a/solution.py
+++ b/solution.py
@@ -129,17 +129,38 @@
 HALVES = 2
 SLOTS = 720
 TILE = 144
-ROOM = 80
+TILES = SLOTS // TILE
+ROOM = 48
 KEEP = 512
 WIDTH = 256
 GROUP = 6144
 HALF = GROUP // HALVES
 HERE = 768
-COMPACT = HALVES * SLOTS
-RECORDS = PLACES * ROOM
 STRIDE = 4096
 ORDER_BITS = 18
-BATCH = 4
+BATCH = 8
+BATCHES = PLACES // BATCH
+ROWS = BATCH * ROOM
+FILLED = 256
+BLOCKS = HALVES * BATCHES
+
+
+def near(step):
+    return min(step, 4 - step)
+
+
+def far_first():
+    steps = [(y, x, k) for y in range(4) for x in range(4) for k in range(2)]
+    steps = sorted(steps[1:], key=lambda s: (-((s[0] == 2) + (s[1] == 2)), -near(s[0]) - near(s[1])))
+    order = [(0, 0, 0)]
+    for s in steps:
+        for one in (s, (-s[0] % 4, -s[1] % 4, s[2])):
+            if one not in order:
+                order.append(one)
+    return order
+
+
+STEPS = far_first()
 MESH_ID = pl.DeviceIdType.MESH
 RELAYED = ((0, 3), (0, 4), (1, 4), (3, 0), (4, 0), (4, 1))
 RELAY_ORDER = (1, 4, 2, 3, 0, 5)
@@ -170,7 +191,7 @@
     out_ref, flag_ref,
     key_ref, dev_ref, rank_ref, meta_ref, cm_ref, had_ref,
     sb_ref, rb_ref, relay_ref, unit_ref, s2_ref, r2_ref, sm_ref, rm_ref,
-    best_ref, rs_ref, rr_ref, tg_ref,
+    pos_ref, full_ref, col_ref, row_ref, top_ref, best_ref, rs_ref, rr_ref, tg_ref,
     zs_sem, zr_sem, ys_sem, yr_sem, us_sem, ur_sem, ms_sem, mr_sem, bs_sem, br_sem, ts_sem, tr_sem, own_sem,
 ):
     z = lax.axis_index("feat")
@@ -197,7 +218,7 @@
     upper = pick(iota((WIDTH, WIDTH + 128), 0) < jnp.where(iota((WIDTH, WIDTH + 128), 1) < WIDTH, iota((WIDTH, WIDTH + 128), 1), WIDTH))
     classes = DEVS + 8
 
-    def rank_block(b, base):
+    def rank_block(h, b, base):
         at = pl.ds(pl.multiple_of(b * WIDTH, WIDTH), WIDTH)
         cl = cluster_ref[0:1, at]
         place = order_ref[0:1, at]
@@ -213,7 +234,7 @@
         slot = jnp.sum(before[DEVS:], axis=0, keepdims=True).astype(I32)
         key_ref[0:1, at] = plane * STRIDE + slot
         dev_ref[0:1, at] = plane * PLACES + q
-        rank_ref[0:1, at] = rank
+        rank_ref[0:1, at] = rank + h * ROOM
         key = (cl << ORDER_BITS) + place
         row = iota((16, WIDTH), 0)
         info = jnp.where(row == 0, key & 255, 0)
@@ -226,15 +247,16 @@
         meta_ref[0:16, at] = info.astype(F32).astype(BF)
         return base + counts[:, WIDTH:]
 
-    base = jnp.zeros((classes, 128), F32)
-    most = jnp.zeros((8, 128), F32)
     per_half = HALF // WIDTH
-    for h in range(HALVES):
-        base = lax.fori_loop(h * per_half, (h + 1) * per_half, rank_block, base)
-        most = jnp.maximum(most, base[DEVS:])
-        base = jnp.concatenate([base[:DEVS], jnp.zeros((8, 128), F32)], axis=0)
-    over = jnp.where(jnp.max(most) > SLOTS, jnp.float32(1), jnp.float32(0))
-    over = jnp.maximum(over, jnp.where(jnp.max(base[:DEVS]) > ROOM, jnp.float32(1), jnp.float32(0)))
+
+    def rank_half(h):
+        count = lax.fori_loop(
+            h * per_half, (h + 1) * per_half, functools.partial(rank_block, h), jnp.zeros((classes, 128), F32), unroll=3
+        )
+        crowded = jnp.where(jnp.max(count[DEVS:]) > SLOTS, jnp.float32(1), jnp.float32(0))
+        return jnp.maximum(crowded, jnp.where(jnp.max(count[:DEVS]) > ROOM, jnp.float32(1), jnp.float32(0)))
+
+    over = rank_half(0)
 
     @pl.when(live)
     def _():
@@ -256,42 +278,54 @@
     def relay_slot(p):
         return jnp.where(p > z, z + p - 3, z + p)
 
-    def direct_copy(i, h, p):
+    def rows_of(t):
+        return pl.ds(pl.multiple_of(t * TILE, TILE), TILE)
+
+    def direct_copy(i, h, t, p):
         return pltpu.make_async_remote_copy(
-            src_ref=sb_ref.at[i, h], dst_ref=rb_ref.at[h, z],
-            send_sem=zs_sem.at[i, h], recv_sem=zr_sem.at[h, z],
+            src_ref=sb_ref.at[i, h, rows_of(t)], dst_ref=rb_ref.at[h, z, rows_of(t)],
+            send_sem=zs_sem.at[i, h, t], recv_sem=zr_sem.at[h, z, t],
             device_id={"feat": p}, device_id_type=MESH_ID)
 
-    def relay_copy(i, h, p):
+    def relay_copy(i, h, t, p):
         slot = relay_slot(p)
         return pltpu.make_async_remote_copy(
-            src_ref=sb_ref.at[i, h], dst_ref=relay_ref.at[slot, h],
-            send_sem=zs_sem.at[i, h], recv_sem=yr_sem.at[slot, h],
+            src_ref=sb_ref.at[i, h, rows_of(t)], dst_ref=relay_ref.at[slot, h, rows_of(t)],
+            send_sem=zs_sem.at[i, h, t], recv_sem=yr_sem.at[slot, h, t],
             device_id={"feat": RELAY}, device_id_type=MESH_ID)
 
-    def forward_copy(r, h):
+    def forward_copy(r, h, t):
         src, dst = RELAYED[r]
         return pltpu.make_async_remote_copy(
-            src_ref=relay_ref.at[r, h], dst_ref=rb_ref.at[h, src],
-            send_sem=ys_sem.at[r, h], recv_sem=zr_sem.at[h, src],
+            src_ref=relay_ref.at[r, h, rows_of(t)], dst_ref=rb_ref.at[h, src, rows_of(t)],
+            send_sem=ys_sem.at[r, h, t], recv_sem=zr_sem.at[h, src, t],
             device_id={"feat": dst}, device_id_type=MESH_ID)
 
-    def unit_copy(q):
+    def seat(j, sign):
+        y, x, k = STEPS[j]
+        y = lax.rem(c // 8 + (4 + sign * y), 4)
+        x = lax.rem(c // 2 % 4 + (4 + sign * x), 4)
+        return y * 8 + x * 2 + lax.rem(c + k, 2)
+
+    def unit_copy(h, j):
+        q = seat(j, 1)
         return pltpu.make_async_remote_copy(
-            src_ref=s2_ref.at[q], dst_ref=r2_ref.at[c],
-            send_sem=us_sem.at[q], recv_sem=ur_sem.at[c],
+            src_ref=s2_ref.at[h, q], dst_ref=r2_ref.at[h, j],
+            send_sem=us_sem.at[h, j], recv_sem=ur_sem.at[h, j],
             device_id={"clus": q}, device_id_type=MESH_ID)
 
-    def meta_copy(q):
+    def meta_copy(j):
+        q = seat(j, 1)
         return pltpu.make_async_remote_copy(
-            src_ref=sm_ref.at[q], dst_ref=rm_ref.at[c],
-            send_sem=ms_sem.at[q], recv_sem=mr_sem.at[c],
+            src_ref=sm_ref.at[q], dst_ref=rm_ref.at[j],
+            send_sem=ms_sem.at[j], recv_sem=mr_sem.at[j],
             device_id={"clus": q}, device_id_type=MESH_ID)
 
-    def best_copy(q):
+    def best_copy(j):
+        q = seat(j, -1)
         return pltpu.make_async_remote_copy(
-            src_ref=rs_ref.at[q], dst_ref=rr_ref.at[c],
-            send_sem=bs_sem.at[q], recv_sem=br_sem.at[c],
+            src_ref=rs_ref.at[j], dst_ref=rr_ref.at[c],
+            send_sem=bs_sem.at[j], recv_sem=br_sem.at[c],
             device_id={"clus": q}, device_id_type=MESH_ID)
 
     def table_copy(p):
@@ -300,82 +334,57 @@
             send_sem=ts_sem.at[p], recv_sem=tr_sem.at[z],
             device_id={"feat": p}, device_id_type=MESH_ID)
 
-    def arrival(ref, sem, index):
+    def arrival(ref, sem, *index):
         return pltpu.make_async_copy(ref.at[index], ref.at[index], sem.at[index])
+
+    def others(action):
+        def one(i, carry):
+            action(lax.rem(c + i, PLACES))
+            return carry
+        lax.fori_loop(1, PLACES, one, 0)
+
+    def chosen(h, p, t):
+        keys = key_ref[0:1, h * HALF:(h + 1) * HALF]
+        return pick(keys == iota((TILE, HALF), 0) + (p * STRIDE + t * TILE))
+
+    sign = (2 * signs_ref[...] - 1).astype(F32)
+
+    def send_half(h):
+        def send_tile(k, carry):
+            t = k // (LIVE - 1)
+            i = k % (LIVE - 1)
+            p = target(i)
+            rows = dot(chosen(h, p, t), x_ref[h * HALF:(h + 1) * HALF, :])
+            sb_ref[i, h, rows_of(t), :] = (rows * sign).astype(BF)
+
+            @pl.when(far(p))
+            def _():
+                relay_copy(i, h, t, p).start()
+
+            @pl.when(jnp.logical_not(far(p)))
+            def _():
+                direct_copy(i, h, t, p).start()
+            return carry
+        lax.fori_loop(0, TILES * (LIVE - 1), send_tile, 0)
 
     @pl.when(live)
     def _():
-        sign = (2 * signs_ref[...] - 1).astype(F32)
-
-        def chosen(h, p, t):
-            keys = key_ref[0:1, h * HALF:(h + 1) * HALF]
-            return pick(keys == iota((TILE, HALF), 0) + (p * STRIDE + t * TILE))
-
-        for h in range(HALVES):
-            def send_chunk(i, carry, h=h):
-                p = target(i)
-
-                def tile(t, carry):
-                    rows = dot(chosen(h, p, t), x_ref[h * HALF:(h + 1) * HALF, :])
-                    sb_ref[i, h, pl.ds(pl.multiple_of(t * TILE, TILE), TILE), :] = (rows * sign).astype(BF)
-                    return carry
-                lax.fori_loop(0, SLOTS // TILE, tile, 0)
-
-                @pl.when(far(p))
-                def _():
-                    relay_copy(i, h, p).start()
-
-                @pl.when(jnp.logical_not(far(p)))
-                def _():
-                    direct_copy(i, h, p).start()
-                return carry
-            lax.fori_loop(0, LIVE - 1, send_chunk, 0)
+        send_half(0)
+
+    over = jnp.maximum(over, rank_half(1))
+
+    @pl.when(live)
+    def _():
+        send_half(1)
 
         for h in range(HALVES):
             def own(t, carry, h=h):
-                at = pl.ds(pl.multiple_of(t * TILE, TILE), TILE)
                 hot = chosen(h, z, t)
                 rows = dot(hot, x_ref[h * HALF:(h + 1) * HALF, :])
-                rb_ref[h, z, at, :] = (rows * sign).astype(BF)
-                info = dot_nt(hot, meta_ref[:, h * HALF:(h + 1) * HALF])
-                cm_ref[pl.ds(pl.multiple_of(h * SLOTS + t * TILE, TILE), TILE), :] = info.astype(BF)
+                rb_ref[h, z, rows_of(t), :] = (rows * sign).astype(BF)
+                cm_ref[h, rows_of(t), :] = dot_nt(hot, meta_ref[:, h * HALF:(h + 1) * HALF]).astype(BF)
                 return carry
-            lax.fori_loop(0, SLOTS // TILE, own, 0)
-
-        unit16 = pick(iota((16, 128), 0) == iota((16, 128), 1))
-        lanes = dot_nt(unit16, cm_ref[...])
-        goal = jnp.where(lanes[4:5] > 0.5, lanes[5:6] * ROOM + lanes[6:7], -1.0).astype(I32)
-
-        def placed(g):
-            return pick(goal == iota((BATCH * ROOM, COMPACT), 0) + g * (BATCH * ROOM))
-
-        def batch_of(i):
-            return lax.rem(lax.div(c, BATCH) + 1 + i, PLACES // BATCH)
-
-        def send_all(copy, g, source, sink, sem):
-            def one(k, carry):
-                q = g * BATCH + k
-
-                @pl.when(q != c)
-                def _():
-                    copy(q).start()
-
-                @pl.when(q == c)
-                def _():
-                    own_copy = pltpu.make_async_copy(source.at[q], sink.at[q], sem)
-                    own_copy.start()
-                    own_copy.wait()
-                return carry
-            lax.fori_loop(0, BATCH, one, 0)
-
-        def send_meta(i, carry):
-            g = batch_of(i)
-            info = dot(placed(g), cm_ref[...])
-            info = jnp.where(iota(info.shape, 1) == 5, over, info)
-            sm_ref[pl.ds(g * BATCH, BATCH)] = info.astype(BF).reshape(BATCH, ROOM, 128)
-            send_all(meta_copy, g, sm_ref, rm_ref, own_sem)
-            return carry
-        lax.fori_loop(0, PLACES // BATCH, send_meta, 0)
+            lax.fori_loop(0, TILES, own, 0)
 
         def walsh(t, carry):
             at = pl.ds(pl.multiple_of(t * 128, 128), 128)
@@ -388,92 +397,160 @@
             return carry
         lax.fori_loop(0, LIVE * WIDTH // 128, walsh, 0)
 
-        for h in range(HALVES):
-            for s in range(LIVE):
-                @pl.when(z != s)
-                def _():
-                    pltpu.make_async_copy(rb_ref.at[h, s], rb_ref.at[h, s], zr_sem.at[h, s]).wait()
-
-            def transform(t, carry, h=h):
-                at = pl.ds(pl.multiple_of(t * TILE, TILE), TILE)
-                block = jnp.concatenate([rb_ref[h, s, at, :] for s in range(LIVE)], axis=1)
+        unit16 = pick(iota((16, 128), 0) == iota((16, 128), 1))
+
+        def goal_of(h):
+            lanes = dot_nt(unit16, cm_ref[h])
+            return jnp.where(lanes[4:5] > 0.5, lanes[5:6] * ROOM + lanes[6:7], -1.0).astype(I32)
+        goals = [goal_of(h) for h in range(HALVES)]
+
+        def placed(h, g):
+            return pick(goals[h] == iota((ROWS, SLOTS), 0) + g * ROWS)
+
+        def send_meta(g, carry):
+            for h in range(HALVES):
+                info = dot(placed(h, g), cm_ref[h])
+                info = jnp.where(iota(info.shape, 1) == 5, over, info)
+                sm_ref[pl.ds(g * BATCH, BATCH), h] = info.astype(BF).reshape(BATCH, ROOM, 128)
+            return carry
+        lax.fori_loop(0, BATCHES, send_meta, 0)
+
+        def keep_own(source, sink):
+            own_copy = pltpu.make_async_copy(source, sink, own_sem)
+            own_copy.start()
+            return own_copy
+        kept = keep_own(sm_ref.at[c], rm_ref.at[0])
+        for j in range(1, PLACES):
+            meta_copy(j).start()
+        kept.wait()
+
+        def transform(h):
+            def tile(t, carry):
+                for s in range(LIVE):
+                    @pl.when(z != s)
+                    def _():
+                        arrived = rb_ref.at[h, s, rows_of(t)]
+                        pltpu.make_async_copy(arrived, arrived, zr_sem.at[h, s, t]).wait()
+                block = jnp.concatenate([rb_ref[h, s, rows_of(t), :] for s in range(LIVE)], axis=1)
                 sketch = dot(block, had_ref[...])
                 total = jnp.sum(sketch * sketch, axis=1, keepdims=True)
-                unit = sketch * lax.rsqrt(total + 1e-06)
-                unit_ref[pl.ds(pl.multiple_of(h * SLOTS + t * TILE, TILE), TILE), :] = unit.astype(BF)
+                unit_ref[h, rows_of(t), :] = (sketch * lax.rsqrt(total + 1e-06)).astype(BF)
                 return carry
-            lax.fori_loop(0, SLOTS // TILE, transform, 0)
-
-        def send_unit(i, carry):
-            g = batch_of(i)
-            rows = dot(placed(g), unit_ref[...])
-            s2_ref[pl.ds(g * BATCH, BATCH)] = rows.astype(BF).reshape(BATCH, ROOM, KEEP)
-            send_all(unit_copy, g, s2_ref, r2_ref, own_sem)
-            return carry
-        lax.fori_loop(0, PLACES // BATCH, send_unit, 0)
-
-        def others(action):
-            def one(i, carry):
-                action(lax.rem(c + i, PLACES))
+            lax.fori_loop(0, TILES, tile, 0)
+
+        def send_units(h):
+            def one(g, carry):
+                rows = dot(placed(h, g), unit_ref[h])
+                s2_ref[h, pl.ds(g * BATCH, BATCH)] = rows.astype(BF).reshape(BATCH, ROOM, KEEP)
                 return carry
-            lax.fori_loop(1, PLACES, one, 0)
-
-        others(lambda q: arrival(rm_ref, mr_sem, q).wait())
-        others(lambda q: arrival(r2_ref, ur_sem, q).wait())
-
-        lanes = dot_nt(unit16, rm_ref[...].reshape(RECORDS, 128))
-        low = (lanes[0:1] + 256.0 * lanes[1:2] + 65536.0 * lanes[2:3]).astype(I32)
-        query_key = low + (lanes[3:4].astype(I32) << 24)
-        query_low = (query_key >> ORDER_BITS) << ORDER_BITS
-        flag = jnp.max(lanes[5:6])
-        many = 8 * ROOM
-        wide = 512
-        for t in range(RECORDS // wide):
-            mine = query_key[:, t * wide:(t + 1) * wide]
-            floor = query_low[:, t * wide:(t + 1) * wide]
-
-            def compare(k, top, t=t, mine=mine, floor=floor):
-                keys = r2_ref[pl.ds(k * 8, 8)].reshape(many, KEEP)
-                info = rm_ref[pl.ds(k * 8, 8)].reshape(many, 128).astype(F32)
-                key = (info[:, 0:1] + 256.0 * info[:, 1:2] + 65536.0 * info[:, 2:3]).astype(I32)
-                key = key + (info[:, 3:4].astype(I32) << 24)
-                key = jnp.where(info[:, 4:5] > 0.5, key, jnp.int32(2 ** 31 - 1))
-                queries = r2_ref[...].reshape(RECORDS, KEEP)[t * wide:(t + 1) * wide]
-                score = dot_nt(keys, queries)
-                score = jnp.where((key < mine) & (key >= floor), score, 0.0)
-                return jnp.maximum(top, jnp.max(score.reshape(many // 8, 8, wide), axis=0))
-            top = lax.fori_loop(0, PLACES // 8, compare, jnp.zeros((8, wide), F32))
-            best_ref[0:1, t * wide:(t + 1) * wide] = jnp.max(top, axis=0, keepdims=True)
-        best_ref[0:1, RECORDS:] = jnp.zeros((1, 128), F32)
-
-        for q in range(PLACES):
-            start = q * ROOM // 128 * 128
-            window = best_ref[0:1, start:start + 256]
-            window = pltpu.roll(jnp.broadcast_to(window, (8, 256)), (256 - (q * ROOM - start)) % 256, 1)
-            rs_ref[q] = window[:, :128]
-
-        def send_best(q):
-            best_copy(q).start()
-        others(send_best)
-        own_copy = pltpu.make_async_copy(rs_ref.at[c], rr_ref.at[c], own_sem)
-        own_copy.start()
-        own_copy.wait()
+            lax.fori_loop(0, BATCHES, one, 0)
+            for j in range(1, PLACES):
+                unit_copy(h, j).start()
+            keep_own(s2_ref.at[h, c], r2_ref.at[h, 0]).wait()
+
+        before = pick(iota((ROWS, ROWS), 0) < iota((ROWS, ROWS), 1))
+
+        def read_meta(b, carry):
+            h = b // BATCHES
+            info = rm_ref[pl.ds(lax.rem(b, BATCHES) * BATCH, BATCH), h].reshape(ROWS, 128)
+            lanes = dot_nt(unit16, info)
+            flag, most = carry
+            rank = dot(lanes.astype(BF), before)[4:5]
+            flag = jnp.maximum(flag, jnp.max(lanes[5:6]))
+            most = jnp.maximum(most, jnp.max(rank + lanes[4:5]))
+            position = jnp.where(lanes[4:5] > 0.5, rank, -1.0).astype(I32)
+            pos_ref[b] = jnp.broadcast_to(position, (8, ROWS))
+            packed = dot(pick(position == iota((FILLED, ROWS), 0)), info)
+            key = (packed[:, 0:1] + 256.0 * packed[:, 1:2] + 65536.0 * packed[:, 2:3]).astype(I32)
+            key = key + (packed[:, 3:4].astype(I32) << 24)
+            key = jnp.where(packed[:, 4:5] > 0.5, key, jnp.int32(2 ** 31 - 1))
+            col_ref[b] = jnp.broadcast_to(key, (FILLED, 128))
+            lanes = dot_nt(unit16, packed.astype(BF))
+            key = (lanes[0:1] + 256.0 * lanes[1:2] + 65536.0 * lanes[2:3]).astype(I32)
+            row_ref[b] = jnp.broadcast_to(key + (lanes[3:4].astype(I32) << 24), (8, FILLED))
+            return flag, most
+
+        def pack(h, k):
+            for j in range(k * BATCH, (k + 1) * BATCH):
+                if j:
+                    arrival(r2_ref, ur_sem, h, j).wait()
+            b = h * BATCHES + k
+            rows = r2_ref[h, k * BATCH:(k + 1) * BATCH].reshape(ROWS, KEEP)
+            full_ref[b] = dot(pick(pos_ref[b, 0:1] == iota((FILLED, ROWS), 0)), rows).astype(BF)
+
+        def match(i, k):
+            mine = row_ref[i, 0:1]
+            floor = (mine >> ORDER_BITS) << ORDER_BITS
+            key = col_ref[k]
+            key = jnp.concatenate([key, key], axis=1)
+            score = dot_nt(full_ref[k], full_ref[i])
+            score = jnp.where((key < mine) & (key >= floor), score, 0.0)
+            return jnp.max(score.reshape(FILLED // 8, 8, FILLED), axis=0)
+
+        def compare(b):
+            def queries(k, top):
+                return jnp.maximum(top, match(b, k))
+            top_ref[b] = lax.fori_loop(0, b + 1, queries, jnp.zeros((8, FILLED), F32), unroll=True)
+
+            def candidates(i, carry):
+                top_ref[i] = jnp.maximum(top_ref[i], match(i, b))
+                return carry
+            lax.fori_loop(0, b, candidates, 0, unroll=True)
+
+        transform(0)
+        send_units(0)
+        for j in range(1, PLACES):
+            arrival(rm_ref, mr_sem, j).wait()
+        flag, most = lax.fori_loop(0, BLOCKS, read_meta, (jnp.float32(0), jnp.float32(0)))
+        flag = jnp.maximum(flag, jnp.where(most > FILLED, jnp.float32(1), jnp.float32(0)))
+        for k in range(BATCHES):
+            pack(0, k)
+            compare(k)
+        transform(1)
+        send_units(1)
+        for k in range(BATCHES):
+            pack(1, k)
+            compare(BATCHES + k)
+        for b in range(BLOCKS):
+            top = jnp.max(top_ref[b], axis=0, keepdims=True)
+            high = top.astype(BF).astype(F32)
+            middle = (top - high).astype(BF).astype(F32)
+            line = iota((16, FILLED), 0)
+            parts = jnp.where(line == 0, high, jnp.where(line == 1, middle, jnp.where(line == 2, top - high - middle, 0.0)))
+            parts = dot(parts.astype(BF), pick(iota((FILLED, ROWS), 0) == pos_ref[b, 0:1]))
+            best_ref[b, :, :ROWS] = jnp.broadcast_to(parts[0:1] + parts[1:2] + parts[2:3], (8, ROWS))
+            best_ref[b, :, ROWS:] = jnp.zeros((8, 128), F32)
+
+        for j in range(PLACES):
+            start = j % BATCH * ROOM
+            left = start // 128 * 128
+            pieces = []
+            for h in range(HALVES):
+                window = best_ref[h * BATCHES + j // BATCH, :, left:left + 256]
+                pieces.append(pltpu.roll(window, (256 - (start - left) + h * ROOM) % 256, 1)[:, :128])
+            lane = iota((8, 128), 1)
+            rs_ref[j] = jnp.where(lane == 127, flag, jnp.where(lane < ROOM, pieces[0], pieces[1]))
+            if j:
+                best_copy(j).start()
+        keep_own(rs_ref.at[0], rr_ref.at[c]).wait()
         others(lambda q: arrival(rr_ref, br_sem, q).wait())
         table = rr_ref[:, 0, :]
-        tg_ref[z] = jnp.where(iota((PLACES, 128), 1) == 127, flag, table)
+        tg_ref[z] = table
         for p in range(8):
             @pl.when(z != p)
             def _():
                 table_copy(p).start()
 
         for h in range(HALVES):
-            def sent(i, carry, h=h):
-                direct_copy(i, h, target(i)).wait_send()
+            def sent(k, carry, h=h):
+                direct_copy(k % (LIVE - 1), h, k // (LIVE - 1), target(k % (LIVE - 1))).wait_send()
                 return carry
-            lax.fori_loop(0, LIVE - 1, sent, 0)
-        others(lambda q: meta_copy(q).wait_send())
-        others(lambda q: unit_copy(q).wait_send())
-        others(lambda q: best_copy(q).wait_send())
+            lax.fori_loop(0, TILES * (LIVE - 1), sent, 0)
+            for j in range(1, PLACES):
+                unit_copy(h, j).wait_send()
+        for j in range(1, PLACES):
+            meta_copy(j).wait_send()
+            best_copy(j).wait_send()
         for p in range(8):
             @pl.when(z != p)
             def _():
@@ -482,12 +559,19 @@
     @pl.when(z == RELAY)
     def _():
         for h in range(HALVES):
-            for r in RELAY_ORDER:
-                pltpu.make_async_copy(relay_ref.at[r, h], relay_ref.at[r, h], yr_sem.at[r, h]).wait()
-                forward_copy(r, h).start()
+            def forward(t, carry, h=h):
+                for r in RELAY_ORDER:
+                    held = relay_ref.at[r, h, rows_of(t)]
+                    pltpu.make_async_copy(held, held, yr_sem.at[r, h, t]).wait()
+                    forward_copy(r, h, t).start()
+                return carry
+            lax.fori_loop(0, TILES, forward, 0)
         for h in range(HALVES):
-            for r in RELAY_ORDER:
-                forward_copy(r, h).wait_send()
+            def forwarded(t, carry, h=h):
+                for r in RELAY_ORDER:
+                    forward_copy(r, h, t).wait_send()
+                return carry
+            lax.fori_loop(0, TILES, forwarded, 0)
 
     for p in range(LIVE):
         @pl.when(z != p)
@@ -520,26 +604,31 @@
             pltpu.VMEM((1, GROUP), I32),
             pltpu.VMEM((1, GROUP), I32),
             pltpu.VMEM((128, GROUP), BF),
-            pltpu.VMEM((COMPACT, 128), BF),
+            pltpu.VMEM((HALVES, SLOTS, 128), BF),
             pltpu.VMEM((LIVE * WIDTH, KEEP), BF),
             pltpu.VMEM((LIVE - 1, HALVES, SLOTS, WIDTH), BF),
             pltpu.VMEM((HALVES, LIVE, SLOTS, WIDTH), BF),
             pltpu.VMEM((len(RELAYED), HALVES, SLOTS, WIDTH), BF),
-            pltpu.VMEM((COMPACT, KEEP), BF),
-            pltpu.VMEM((PLACES, ROOM, KEEP), BF),
-            pltpu.VMEM((PLACES, ROOM, KEEP), BF),
-            pltpu.VMEM((PLACES, ROOM, 128), BF),
-            pltpu.VMEM((PLACES, ROOM, 128), BF),
-            pltpu.VMEM((1, RECORDS + 128), F32),
+            pltpu.VMEM((HALVES, SLOTS, KEEP), BF),
+            pltpu.VMEM((HALVES, PLACES, ROOM, KEEP), BF),
+            pltpu.VMEM((HALVES, PLACES, ROOM, KEEP), BF),
+            pltpu.VMEM((PLACES, HALVES, ROOM, 128), BF),
+            pltpu.VMEM((PLACES, HALVES, ROOM, 128), BF),
+            pltpu.VMEM((BLOCKS, 8, ROWS), I32),
+            pltpu.VMEM((BLOCKS, FILLED, KEEP), BF),
+            pltpu.VMEM((BLOCKS, FILLED, 128), I32),
+            pltpu.VMEM((BLOCKS, 8, FILLED), I32),
+            pltpu.VMEM((BLOCKS, 8, FILLED), F32),
+            pltpu.VMEM((BLOCKS, 8, ROWS + 128), F32),
             pltpu.VMEM((PLACES, 8, 128), F32),
             pltpu.VMEM((PLACES, 8, 128), F32),
             pltpu.VMEM((LIVE, PLACES, 128), F32),
-            dma((LIVE - 1, HALVES)),
-            dma((HALVES, LIVE)),
-            dma((len(RELAYED), HALVES)),
-            dma((len(RELAYED), HALVES)),
-            dma((PLACES,)),
-            dma((PLACES,)),
+            dma((LIVE - 1, HALVES, TILES)),
+            dma((HALVES, LIVE, TILES)),
+            dma((len(RELAYED), HALVES, TILES)),
+            dma((len(RELAYED), HALVES, TILES)),
+            dma((HALVES, PLACES)),
+            dma((HALVES, PLACES)),
             dma((PLACES,)),
             dma((PLACES,)),
             dma((PLACES,)),

time: 152 us -> 113 us (0.74)
  Pallas kernels: 151 us -> 111 us
    pallas_call x1, Pallas kernels: 151 us -> 111 us  [local(): pl.pallas_call(fast_kernel, out_shape=(jax.ShapeDtypeStruct((1, HERE), F3...]
where the time goes in v2:
time: 113 us
  Pallas kernels  111 us (98%)
    pallas_call x1, Pallas kernels, local(): pl.pallas_call(fast_kernel, out_shape=(jax.ShapeDtypeStruct((1, HERE), F3...  111 us

profile of v2, /device:TPU:1, one launch (start us, length us, event | category | flops | bytes accessed | tf_op | source)
XLA Modules:
  0.0 112.8 jit_solution(2312336170351059393)
XLA Ops:
  0.0 0.0 copy-start
  0.0 0.0 copy-start.10
  0.0 0.0 copy-start.4
  0.0 111.3 %shard_map.77 = (f32[1,768]{1,0:T(1,128)S(1)}, f32[1,128]{1,0:T(1,128)}) custom-call(bf16[6144,256]{1,0:T(8,128)(2,1)} %x_ref.1, s32[1,256]{1,0:T(1,128)} %bitcast.62, s32[1,512]{1,0:T(1,128)} %bitcast.61, s32[1,6144]{1,0:T(1,128)} %bitcast.59, s32[1,6144]{1,0:T(1,128)} %bitcast.60), custom_call_target="tpu_custom_call" | custom-call | tf_op jit(solution)/shard_map/pallas_call | solution.py:597
  112.0 0.0 copy-done
  112.0 0.0 copy-done.10
  112.0 0.0 copy-done.4
  112.0 0.3 conditional.1
  112.3 0.6 copy.85
Async XLA Ops:
  0.0 112.0 %copy-start = (bf16[6144,256]{1,0:T(8,128)(2,1)S(1)}, bf16[6144,256]{1,0:T(8,128)(2,1)}, u32[]{:S(2)}) copy-start(bf16[6144,256]{1,0:T(8,128)(2,1)} %x_ref.1) | copy-start | bytes 9437188
  0.0 112.0 %copy-start.10 = (s32[256]{0:T(256)S(1)}, s32[256]{0:T(256)}, u32[]{:S(2)}) copy-start(s32[256]{0:T(256)} %param.12) | copy-start | bytes 3076
  0.0 112.0 %copy-start.4 = (s32[512]{0:T(512)S(1)}, s32[512]{0:T(512)}, u32[]{:S(2)}) copy-start(s32[512]{0:T(512)} %param.13) | copy-start | bytes 6148

commit v3 on v2

--- a/solution.py
+++ b/solution.py
@@ -123,7 +123,6 @@
 
 
 LIVE = 5
-RELAY = 6
 PLACES = 32
 DEVS = LIVE * PLACES
 HALVES = 2
@@ -131,6 +130,7 @@
 TILE = 144
 TILES = SLOTS // TILE
 ROOM = 48
+STRAIGHT = 1
 KEEP = 512
 WIDTH = 256
 GROUP = 6144
@@ -162,8 +162,6 @@
 
 STEPS = far_first()
 MESH_ID = pl.DeviceIdType.MESH
-RELAYED = ((0, 3), (0, 4), (1, 4), (3, 0), (4, 0), (4, 1))
-RELAY_ORDER = (1, 4, 2, 3, 0, 5)
 BF = jnp.bfloat16
 F32 = jnp.float32
 I32 = jnp.int32
@@ -203,9 +201,10 @@
         def _():
             pl.semaphore_signal(barrier, inc=1, device_id={"feat": s}, device_id_type=MESH_ID)
 
-    @pl.when((z == 0) | (z == 1) | (z == 3) | (z == 4))
-    def _():
-        pl.semaphore_signal(barrier, inc=1, device_id={"feat": RELAY}, device_id_type=MESH_ID)
+    for a, b in ((0, 3), (0, 4), (1, 4)):
+        @pl.when((z == a) | (z == b))
+        def _():
+            pl.semaphore_signal(barrier, inc=1, device_id={"feat": a + b + 2}, device_id_type=MESH_ID)
 
     @pl.when(live)
     def _():
@@ -262,9 +261,9 @@
     def _():
         pl.semaphore_wait(barrier, 7 + PLACES - 1)
 
-    @pl.when(z == RELAY)
+    @pl.when(jnp.logical_not(live))
     def _():
-        pl.semaphore_wait(barrier, 4)
+        pl.semaphore_wait(barrier, 2)
 
     def target(i):
         down = 4 - i
@@ -272,11 +271,9 @@
         up = jnp.where(i >= z, i + 1, i)
         return jnp.where(z < 2, down, up)
 
-    def far(p):
-        return (p - z >= 3) | (z - p >= 3)
-
-    def relay_slot(p):
-        return jnp.where(p > z, z + p - 3, z + p)
+    def far(p, h, t):
+        steps = jnp.where(p > z, p - z, z - p)
+        return (steps >= 4) | ((steps == 3) & (h * TILES + t < HALVES * TILES - STRAIGHT))
 
     def rows_of(t):
         return pl.ds(pl.multiple_of(t * TILE, TILE), TILE)
@@ -288,14 +285,16 @@
             device_id={"feat": p}, device_id_type=MESH_ID)
 
     def relay_copy(i, h, t, p):
-        slot = relay_slot(p)
+        slot = jnp.where(p > z, 0, 1)
         return pltpu.make_async_remote_copy(
             src_ref=sb_ref.at[i, h, rows_of(t)], dst_ref=relay_ref.at[slot, h, rows_of(t)],
             send_sem=zs_sem.at[i, h, t], recv_sem=yr_sem.at[slot, h, t],
-            device_id={"feat": RELAY}, device_id_type=MESH_ID)
+            device_id={"feat": z + p + 2}, device_id_type=MESH_ID)
 
     def forward_copy(r, h, t):
-        src, dst = RELAYED[r]
+        low = z // 7
+        high = z - 2 - low
+        src, dst = (low, high) if r == 0 else (high, low)
         return pltpu.make_async_remote_copy(
             src_ref=relay_ref.at[r, h, rows_of(t)], dst_ref=rb_ref.at[h, src, rows_of(t)],
             send_sem=ys_sem.at[r, h, t], recv_sem=zr_sem.at[h, src, t],
@@ -357,11 +356,11 @@
             rows = dot(chosen(h, p, t), x_ref[h * HALF:(h + 1) * HALF, :])
             sb_ref[i, h, rows_of(t), :] = (rows * sign).astype(BF)
 
-            @pl.when(far(p))
+            @pl.when(far(p, h, t))
             def _():
                 relay_copy(i, h, t, p).start()
 
-            @pl.when(jnp.logical_not(far(p)))
+            @pl.when(jnp.logical_not(far(p, h, t)))
             def _():
                 direct_copy(i, h, t, p).start()
             return carry
@@ -499,6 +498,8 @@
 
         transform(0)
         send_units(0)
+        transform(1)
+        send_units(1)
         for j in range(1, PLACES):
             arrival(rm_ref, mr_sem, j).wait()
         flag, most = lax.fori_loop(0, BLOCKS, read_meta, (jnp.float32(0), jnp.float32(0)))
@@ -506,8 +507,6 @@
         for k in range(BATCHES):
             pack(0, k)
             compare(k)
-        transform(1)
-        send_units(1)
         for k in range(BATCHES):
             pack(1, k)
             compare(BATCHES + k)
@@ -556,22 +555,25 @@
             def _():
                 table_copy(p).wait_send()
 
-    @pl.when(z == RELAY)
+    @pl.when(jnp.logical_not(live))
     def _():
-        for h in range(HALVES):
-            def forward(t, carry, h=h):
-                for r in RELAY_ORDER:
-                    held = relay_ref.at[r, h, rows_of(t)]
-                    pltpu.make_async_copy(held, held, yr_sem.at[r, h, t]).wait()
-                    forward_copy(r, h, t).start()
-                return carry
-            lax.fori_loop(0, TILES, forward, 0)
-        for h in range(HALVES):
-            def forwarded(t, carry, h=h):
-                for r in RELAY_ORDER:
-                    forward_copy(r, h, t).wait_send()
-                return carry
-            lax.fori_loop(0, TILES, forwarded, 0)
+        def passed(r, h, t, action):
+            @pl.when((z == 6) | (h * TILES + t < HALVES * TILES - STRAIGHT))
+            def _():
+                action(r, h, t)
+
+        def pass_on(r, h, t):
+            held = relay_ref.at[r, h, rows_of(t)]
+            pltpu.make_async_copy(held, held, yr_sem.at[r, h, t]).wait()
+            forward_copy(r, h, t).start()
+
+        for action in (pass_on, lambda r, h, t: forward_copy(r, h, t).wait_send()):
+            for h in range(HALVES):
+                def tile(t, carry, h=h, action=action):
+                    for r in range(2):
+                        passed(r, h, t, action)
+                    return carry
+                lax.fori_loop(0, TILES, tile, 0)
 
     for p in range(LIVE):
         @pl.when(z != p)
@@ -608,7 +610,7 @@
             pltpu.VMEM((LIVE * WIDTH, KEEP), BF),
             pltpu.VMEM((LIVE - 1, HALVES, SLOTS, WIDTH), BF),
             pltpu.VMEM((HALVES, LIVE, SLOTS, WIDTH), BF),
-            pltpu.VMEM((len(RELAYED), HALVES, SLOTS, WIDTH), BF),
+            pltpu.VMEM((2, HALVES, SLOTS, WIDTH), BF),
             pltpu.VMEM((HALVES, SLOTS, KEEP), BF),
             pltpu.VMEM((HALVES, PLACES, ROOM, KEEP), BF),
             pltpu.VMEM((HALVES, PLACES, ROOM, KEEP), BF),
@@ -625,8 +627,8 @@
             pltpu.VMEM((LIVE, PLACES, 128), F32),
             dma((LIVE - 1, HALVES, TILES)),
             dma((HALVES, LIVE, TILES)),
-            dma((len(RELAYED), HALVES, TILES)),
-            dma((len(RELAYED), HALVES, TILES)),
+            dma((2, HALVES, TILES)),
+            dma((2, HALVES, TILES)),
             dma((HALVES, PLACES)),
             dma((HALVES, PLACES)),
             dma((PLACES,)),

time: 113 us -> 106 us (0.938)
  Pallas kernels: 111 us -> 104 us
    pallas_call x1, Pallas kernels: 111 us -> 104 us  [local(): pl.pallas_call(fast_kernel, out_shape=(jax.ShapeDtypeStruct((1, HERE), F3...]
where the time goes in v3:
time: 106 us
  Pallas kernels  104 us (98%)
    pallas_call x1, Pallas kernels, local(): pl.pallas_call(fast_kernel, out_shape=(jax.ShapeDtypeStruct((1, HERE), F3...  104 us

profile of v3, /device:TPU:1, one launch (start us, length us, event | category | flops | bytes accessed | tf_op | source)
XLA Modules:
  0.0 105.9 jit_solution(4096832201486408593)
XLA Ops:
  0.0 0.0 copy-start
  0.0 0.0 copy-start.10
  0.0 0.0 copy-start.4
  0.0 104.4 %shard_map.77 = (f32[1,768]{1,0:T(1,128)S(1)}, f32[1,128]{1,0:T(1,128)}) custom-call(bf16[6144,256]{1,0:T(8,128)(2,1)} %x_ref.1, s32[1,256]{1,0:T(1,128)} %bitcast.62, s32[1,512]{1,0:T(1,128)} %bitcast.61, s32[1,6144]{1,0:T(1,128)} %bitcast.59, s32[1,6144]{1,0:T(1,128)} %bitcast.60), custom_call_target="tpu_custom_call" | custom-call | tf_op jit(solution)/shard_map/pallas_call | solution.py:599
  105.0 0.0 copy-done
  105.0 0.0 copy-done.10
  105.0 0.0 copy-done.4
  105.0 0.3 conditional.1
  105.3 0.6 copy.85
Async XLA Ops:
  0.0 105.0 %copy-start = (bf16[6144,256]{1,0:T(8,128)(2,1)S(1)}, bf16[6144,256]{1,0:T(8,128)(2,1)}, u32[]{:S(2)}) copy-start(bf16[6144,256]{1,0:T(8,128)(2,1)} %x_ref.1) | copy-start | bytes 9437188
  0.0 105.0 %copy-start.10 = (s32[256]{0:T(256)S(1)}, s32[256]{0:T(256)}, u32[]{:S(2)}) copy-start(s32[256]{0:T(256)} %param.12) | copy-start | bytes 3076
  0.0 105.0 %copy-start.4 = (s32[512]{0:T(512)S(1)}, s32[512]{0:T(512)}, u32[]{:S(2)}) copy-start(s32[512]{0:T(512)} %param.13) | copy-start | bytes 6148

commit v4 on v3

--- a/solution.py
+++ b/solution.py
@@ -185,17 +185,19 @@
 
 
 def fast_kernel(
-    x_ref, signs_ref, coords_ref, cluster_ref, order_ref,
+    hbm_ref, signs_ref, coords_ref, cluster_ref, order_ref,
     out_ref, flag_ref,
     key_ref, dev_ref, rank_ref, meta_ref, cm_ref, had_ref,
     sb_ref, rb_ref, relay_ref, unit_ref, s2_ref, r2_ref, sm_ref, rm_ref,
     pos_ref, full_ref, col_ref, row_ref, top_ref, best_ref, rs_ref, rr_ref, tg_ref,
-    zs_sem, zr_sem, ys_sem, yr_sem, us_sem, ur_sem, ms_sem, mr_sem, bs_sem, br_sem, ts_sem, tr_sem, own_sem,
+    zs_sem, zr_sem, ys_sem, yr_sem, us_sem, ur_sem, ms_sem, mr_sem, bs_sem, br_sem, ts_sem, tr_sem, own_sem, x_ref, x_sem,
 ):
     z = lax.axis_index("feat")
     c = lax.axis_index("clus")
     live = z < LIVE
     barrier = pltpu.get_barrier_semaphore()
+    fetch = pltpu.make_async_copy(hbm_ref, x_ref, x_sem)
+    fetch.start()
     for s in range(LIVE):
         @pl.when(z != s)
         def _():
@@ -256,6 +258,7 @@
         return jnp.maximum(crowded, jnp.where(jnp.max(count[:DEVS]) > ROOM, jnp.float32(1), jnp.float32(0)))
 
     over = rank_half(0)
+    fetch.wait()
 
     @pl.when(live)
     def _():
@@ -599,7 +602,7 @@
     best, flag = pl.pallas_call(
         fast_kernel,
         out_shape=(jax.ShapeDtypeStruct((1, HERE), F32), jax.ShapeDtypeStruct((1, 128), F32)),
-        in_specs=[vmem] * 5,
+        in_specs=[pl.BlockSpec(memory_space=pl.ANY)] + [vmem] * 4,
         out_specs=(vmem, vmem),
         scratch_shapes=[
             pltpu.VMEM((1, GROUP), I32),
@@ -638,6 +641,8 @@
             dma((8,)),
             dma((LIVE,)),
             dma,
+            pltpu.VMEM((GROUP, WIDTH), BF),
+            dma,
         ],
         compiler_params=pltpu.CompilerParams(
             collective_id=0, has_side_effects=True, vmem_limit_bytes=56 * 1024 * 1024

time: 106 us -> 105 us (level)
    pallas_call x1, Pallas kernels: 104 us -> 103 us  [local(): pl.pallas_call(fast_kernel, out_shape=(jax.ShapeDtypeStruct((1, HERE), F3...]
where the time goes in v4:
time: 105 us
  Pallas kernels  103 us (98%)
    pallas_call x1, Pallas kernels, local(): pl.pallas_call(fast_kernel, out_shape=(jax.ShapeDtypeStruct((1, HERE), F3...  103 us

profile of v4, /device:TPU:1, one launch (start us, length us, event | category | flops | bytes accessed | tf_op | source)
XLA Modules:
  0.0 104.7 jit_solution(15249279844996651501)
XLA Ops:
  0.0 0.0 copy-start
  0.0 0.0 copy-start.10
  0.0 0.0 copy-start.4
  0.0 103.2 %shard_map.77 = (f32[1,768]{1,0:T(1,128)S(1)}, f32[1,128]{1,0:T(1,128)}) custom-call(bf16[6144,256]{1,0:T(8,128)(2,1)} %hbm_ref.1, s32[1,256]{1,0:T(1,128)} %bitcast.62, s32[1,512]{1,0:T(1,128)} %bitcast.61, s32[1,6144]{1,0:T(1,128)} %bitcast.59, s32[1,6144]{1,0:T(1,128)} %bitcast.60), custom_call_target="tpu_custom_call" | custom-call | tf_op jit(solution)/shard_map/pallas_call | solution.py:602
  103.8 0.0 copy-done
  103.8 0.0 copy-done.10
  103.8 0.0 copy-done.4
  103.9 0.3 conditional.1
  104.1 0.6 copy.85
Async XLA Ops:
  0.0 103.8 %copy-start = (bf16[6144,256]{1,0:T(8,128)(2,1)S(1)}, bf16[6144,256]{1,0:T(8,128)(2,1)}, u32[]{:S(2)}) copy-start(bf16[6144,256]{1,0:T(8,128)(2,1)} %hbm_ref.1) | copy-start | bytes 9437188
  0.0 103.8 %copy-start.10 = (s32[256]{0:T(256)S(1)}, s32[256]{0:T(256)}, u32[]{:S(2)}) copy-start(s32[256]{0:T(256)} %param.12) | copy-start | bytes 3076
  0.0 103.8 %copy-start.4 = (s32[512]{0:T(512)S(1)}, s32[512]{0:T(512)}, u32[]{:S(2)}) copy-start(s32[512]{0:T(512)} %param.13) | copy-start | bytes 6148
